TPU v7x, 256 devices: a whole 4x4x8 slice. The times are simulated.
256 devices in a mesh: bricks: 32 (over y, x, core), scenes: 8 (over z).
Axes of the slice: x: 4, y: 4, z: 8, core: 2. Of those that a mesh axis runs over, the one named last changes fastest.
Arguments:
- features: bfloat16 [8, 256, 64, 512], P('scenes', 'bricks'), may hold values from -6 to 6
- cotangent: bfloat16 [8, 256, 64, 512], P('scenes', 'bricks'), may hold values from -6 to 6
- neighbours: int32 [8, 256, 26], P('scenes', 'bricks'), may hold values from -1 to 255, as said below
- mask: int32 [8, 256, 512], P('scenes', 'bricks'), may hold values from 0 to 1, as said below
- weight_one: bfloat16 [64, 1728], replicated, may hold values from -0.15625 to 0.15625
- bias_one: float32 [64], replicated, may hold values from -3 to 3
- weight_two: bfloat16 [64, 1728], replicated, may hold values from -0.15625 to 0.15625
- bias_two: float32 [64], replicated, may hold values from -3 to 3
Outputs:
- output: bfloat16 [8, 256, 64, 512], P('scenes', 'bricks')
- grad_features: bfloat16 [8, 256, 64, 512], P('scenes', 'bricks')
- grad_weight_one: float32 [64, 1728], replicated
- grad_weight_two: float32 [64, 1728], replicated
- grad_bias_one: float32 [64], replicated
- grad_bias_two: float32 [64], replicated
Inputs may be any that keep to these rules, and one draw needn't show every extreme that they name: `neighbours`: the bricks are cells of a lattice of 2 x 2 x (2 times the bricks axis's size) cells. Index d of the bricks axis holds the cells with third coordinate in d * 2 .. d * 2 + 1; brick g lies on index g // 8, and its slot s = g % 8 is 2 * 2 x + 2 y + (z - d * 2). Some cells are inactive. Entry j of brick g names the brick at the j-th non-zero offset, or is -1 where that cell is inactive or outside the lattice or where g is inactive. g names h at an offset exactly when h names g at the opposite offset. Inactive bricks have mask 0 on every voxel.
All inputs are finite; a program needn't handle non-finite values.
Results may differ from a plain program's by a relative error of at most 0.015.
Values may be sent and summed in bfloat16 or wider, within the bound.
A program may use at most 128 MiB of HBM per device.

v0:
```python
import jax
import jax.numpy as jnp
from jax import lax
from jax.sharding import PartitionSpec as P

E = 8


def padded_2(shard, sides, width):
    for axis, dim in sides:
        devices, length = (lax.axis_size(axis), shard.shape[dim])
        up = [(i, (i + 1) % devices) for i in range(devices - 1)]
        down = [(j, i) for i, j in up]
        last = lax.slice_in_dim(shard, length - width, length, axis=dim)
        first = lax.slice_in_dim(shard, 0, width, axis=dim)
        before = lax.ppermute(last, axis, up)
        after = lax.ppermute(first, axis, down)
        shard = jnp.concatenate([before, shard, after], axis=dim)
    return shard


def tap_list():
    offsets = []
    for step_x in (-1, 0, 1):
        for step_y in (-1, 0, 1):
            for step_z in (-1, 0, 1):
                offsets.append((step_x, step_y, step_z))
    return offsets


def side_list():
    return [offset for offset in tap_list() if offset != (0, 0, 0)]


def brick_faces(cube):
    edge_len = cube.shape[-1]
    return jnp.stack(
        [
            cube[:, :, 0],
            cube[:, :, edge_len - 1],
            cube[:, :, :, 0],
            cube[:, :, :, edge_len - 1],
            cube[:, :, :, :, 0],
            cube[:, :, :, :, edge_len - 1],
        ],
        axis=1,
    )


def cut_range(step_by, edge_len):
    if step_by == -1:
        return slice(edge_len - 1, edge_len)
    if step_by == 1:
        return slice(0, 1)
    return slice(0, edge_len)


def face_number(offset):
    if offset[0] != 0:
        return 0 if offset[0] == 1 else 1
    if offset[1] != 0:
        return 2 if offset[1] == 1 else 3
    return 4 if offset[2] == 1 else 5


def face_piece(face_rows, offset, edge_len):
    if offset[0] != 0:
        return face_rows[:, :, cut_range(offset[1], edge_len), cut_range(offset[2], edge_len)][
            :, :, None
        ]
    if offset[1] != 0:
        return face_rows[:, :, :, cut_range(offset[2], edge_len)][:, :, :, None]
    return face_rows[:, :, :, :, None]


def assemble(cube, face_pool, lookup):
    pieces = {(0, 0, 0): cube}
    edge_len = cube.shape[2]
    for number, offset in enumerate(side_list()):
        face_rows = face_pool[lookup[:, number], face_number(offset)]
        pieces[offset] = face_piece(face_rows, offset, edge_len)
    planes = []
    for step_x in (-1, 0, 1):
        row_list = []
        for step_y in (-1, 0, 1):
            row_list.append(
                jnp.concatenate([pieces[step_x, step_y, step_z] for step_z in (-1, 0, 1)], axis=4)
            )
        planes.append(jnp.concatenate(row_list, axis=3))
    return jnp.concatenate(planes, axis=2)


def routing(neighbours, bricks_dev, depth):
    own_index = lax.axis_index("bricks")
    valid_entry = neighbours >= 0
    owners = jnp.where(valid_entry, neighbours // bricks_dev, own_index)
    slot_of = neighbours % bricks_dev
    local_row = neighbours - own_index * bricks_dev
    lower_row = bricks_dev + slot_of // depth
    upper_row = bricks_dev + 4 + slot_of // depth
    lookup = jnp.where(
        owners == own_index, local_row, jnp.where(owners < own_index, lower_row, upper_row)
    )
    lookup = jnp.where(valid_entry, lookup, bricks_dev + 8)
    return lookup


def with_halo(cube, lookup, depth):
    channels, edge_len = (cube.shape[1], cube.shape[2])
    own_faces = brick_faces(cube)
    columns = cube.reshape(4, depth, channels, edge_len, edge_len, edge_len)
    lowest = columns[:, 0, :, :, :, 0]
    highest = columns[:, depth - 1, :, :, :, edge_len - 1]
    padded = padded_2(jnp.stack([lowest, highest], axis=0), (("bricks", 0),), 1)
    below_plane = padded[0]
    above_plane = padded[3]
    blank = jnp.zeros((4, channels, edge_len, edge_len, edge_len - 1), cube.dtype)
    below_cube = jnp.concatenate([blank, below_plane[:, :, :, :, None]], axis=4)
    above_cube = jnp.concatenate([above_plane[:, :, :, :, None], blank], axis=4)
    face_pool = jnp.concatenate(
        [
            own_faces,
            brick_faces(below_cube),
            brick_faces(above_cube),
            jnp.zeros((1, 6, channels, edge_len, edge_len), cube.dtype),
        ],
        axis=0,
    )
    return assemble(cube, face_pool, lookup)


def kernel_of(weight):
    channels = weight.shape[0]
    return weight.reshape(channels, 3, 3, 3, channels).transpose(0, 4, 1, 2, 3)


def forward_conv(padded, weight):
    result = lax.conv_general_dilated(
        padded,
        kernel_of(weight),
        (1, 1, 1),
        "VALID",
        dimension_numbers=("NCDHW", "OIDHW", "NCDHW"),
        preferred_element_type=jnp.float32,
    )
    return result.reshape(result.shape[0], result.shape[1], -1)


def transposed_conv(padded, weight):
    flipped = kernel_of(weight).transpose(1, 0, 2, 3, 4)[:, :, ::-1, ::-1, ::-1]
    result = lax.conv_general_dilated(
        padded,
        flipped,
        (1, 1, 1),
        "VALID",
        dimension_numbers=("NCDHW", "OIDHW", "NCDHW"),
        preferred_element_type=jnp.float32,
    )
    return result.reshape(result.shape[0], result.shape[1], -1)


def weight_grad(values, padded):
    edge_len = padded.shape[2] - 2
    channels = values.shape[1]
    cube_vals = values.reshape(values.shape[0], channels, edge_len, edge_len, edge_len)
    result = lax.conv_general_dilated(
        padded,
        cube_vals,
        (1, 1, 1),
        "VALID",
        dimension_numbers=("CNDHW", "IODHW", "NCDHW"),
        preferred_element_type=jnp.float32,
    )
    return result.transpose(1, 2, 3, 4, 0).reshape(channels, 27 * channels)


def silu_slope(values):
    sigma = jax.nn.sigmoid(values)
    return sigma * (1.0 + values * (1.0 - sigma))


def local(features, cotangent, neighbours, mask, weight_one, bias_one, weight_two, bias_two):
    features = features[0]
    cotangent = cotangent[0]
    neighbours = neighbours[0]
    mask = mask[0]
    bricks_dev, channels = (features.shape[0], features.shape[1])
    depth = bricks_dev // 4
    lookup = routing(neighbours, bricks_dev, depth)
    live_mask = mask.astype(jnp.float32)[:, None, :]
    masked = features * mask.astype(jnp.bfloat16)[:, None, :]

    def cube_of(values):
        return values.reshape(bricks_dev, channels, E, E, E)

    masked_pad = with_halo(cube_of(masked), lookup, depth)
    first = live_mask * (forward_conv(masked_pad, weight_one) + bias_one[None, :, None])
    hidden = jax.nn.silu(first).astype(jnp.bfloat16)
    hidden_pad = with_halo(cube_of(hidden), lookup, depth)
    second = live_mask * (forward_conv(hidden_pad, weight_two) + bias_two[None, :, None])
    summed = second + masked.astype(jnp.float32)
    output = jax.nn.silu(summed).astype(jnp.bfloat16)
    grad_summed = (cotangent.astype(jnp.float32) * silu_slope(summed) * live_mask).astype(
        jnp.bfloat16
    )
    grad_pad = with_halo(cube_of(grad_summed), lookup, depth)
    grad_weight_two = weight_grad(grad_summed, hidden_pad)
    grad_bias_two = jnp.sum(grad_summed.astype(jnp.float32), axis=(0, 2))
    grad_first = (transposed_conv(grad_pad, weight_two) * silu_slope(first) * live_mask).astype(
        jnp.bfloat16
    )
    first_pad = with_halo(cube_of(grad_first), lookup, depth)
    grad_weight_one = weight_grad(grad_first, masked_pad)
    grad_bias_one = jnp.sum(grad_first.astype(jnp.float32), axis=(0, 2))
    grad_features = (
        live_mask * (grad_summed.astype(jnp.float32) + transposed_conv(first_pad, weight_one))
    ).astype(jnp.bfloat16)
    grad_weight_one, grad_weight_two, grad_bias_one, grad_bias_two = lax.psum(
        (grad_weight_one, grad_weight_two, grad_bias_one, grad_bias_two), ("bricks", "scenes")
    )
    return (
        output[None],
        grad_features[None],
        grad_weight_one,
        grad_weight_two,
        grad_bias_one,
        grad_bias_two,
    )


def solution(mesh):
    return jax.shard_map(
        local,
        mesh=mesh,
        in_specs=(
            P("scenes", "bricks", None, None),
            P("scenes", "bricks", None, None),
            P("scenes", "bricks", None),
            P("scenes", "bricks", None),
            P(),
            P(),
            P(),
            P(),
        ),
        out_specs=(
            P("scenes", "bricks", None, None),
            P("scenes", "bricks", None, None),
            P(),
            P(),
            P(),
            P(),
        ),
        check_vma=False,
    )
```

profile of v0, /device:TPU:1, one launch (start us, length us, event | category | flops | bytes accessed | tf_op | source)
XLA Modules:
  0.0 525.2 jit_solution(13061476586774667654)
XLA Ops:
  8.8 1.6 copy.2598
  11.5 5.1 collective-permute-start.1
  16.7 1.9 collective-permute-start
  24.6 1.7 copy.2723
  26.3 2.0 copy.2876
  56.7 1.5 slice.977
  70.2 9.9 %maximum_maximum_fusion.4 = bf16[8,64,10,10,10]{1,0,4,3,2:T(8,128)(2,1)S(1)} fusion(bf16[8,64,1,1,1]{1,0,4,3,2:T(8,128)(2,1)S(1)} %get-tuple-element.80, bf16[8,64,1,1,8]{1,0,4,3,2:T(8,128)(2,1)S(1)} %get-tuple-element.68, bf16[8,64,1,1,1]{1,0,4,3,2:T(8,128)(2,1)S(1)} %get-tuple-element.81, bf16[8,64,1,8,1]{1,0,4,3,2:T(8,128)(2,1)S(1)} %get-tuple-element.70, ...), kind=kLoop, calls=%fused_computation.119 | loop fusion | flops 13312000 | bytes 2048000 | tf_op jit(solution)/shard_map/concatenate | solution.py:90
  80.2 8.5 %multiply_convert_fusion.5 = (bf16[8,64,8,8,8]{1,0,4,3,2:T(8,128)(2,1)S(1)}, f32[8,64,8,8,8]{1,0,4,3,2:T(8,128)S(1)}) fusion(f32[64]{0:T(128)S(1)} %copy-done.155, f32[8,8,8,8]{0,3,2,1:T(8,128)S(1)} %bitcast.760, bf16[8,64,10,10,10]{1,0,4,3,2:T(8,128)(2,1)S(1)} %maximum_maximum_fusion.4, bf16[64,3,3,3,64]{4,3,2,1,0:T(4,128)(2,1)S(1)} %copy-done.34), kind=kOutput, calls=%fused_computation.116 | convolution fusion | flops 907804672 | bytes 2834688 | tf_op jit(solution)/shard_map/conv_general_dilated | solution.py:138
  91.3 1.9 collective-permute-start.2
  93.4 2.4 collective-permute-start.3
  96.0 3.0 collective-permute-done.3
  144.9 9.9 %maximum_maximum_fusion.5 = bf16[8,64,10,10,10]{1,0,4,3,2:T(8,128)(2,1)S(1)} fusion(bf16[8,64,1,1,1]{1,0,4,3,2:T(8,128)(2,1)S(1)} %bitcast.820, bf16[8,64,1,1,8]{1,0,4,3,2:T(8,128)(2,1)S(1)} %bitcast.784, bf16[8,64,1,1,1]{1,0,4,3,2:T(8,128)(2,1)S(1)} %bitcast.821, bf16[8,64,1,8,1]{1,0,4,3,2:T(8,128)(2,1)S(1)} %bitcast.776, ...), kind=kLoop, calls=%fused_computation.120 | loop fusion | flops 13312000 | bytes 2048000 | tf_op jit(solution)/shard_map/concatenate | solution.py:90
  154.9 8.8 %multiply_convert_fusion.3 = (bf16[8,64,8,8,8]{1,0,4,3,2:T(8,128)(2,1)S(1)}, f32[8,64,8,8,8]{1,0,4,3,2:T(8,128)S(1)}) fusion(f32[8,64,8,8,8]{1,0,4,3,2:T(8,128)S(1)} %bitcast.744, bf16[8,64,8,8,8]{1,0,4,3,2:T(8,128)(2,1)S(1)} %copy-done.14, f32[64]{0:T(128)S(1)} %copy-done.152, f32[8,8,8,8]{0,3,2,1:T(8,128)S(1)} %bitcast.761, ...), kind=kOutput, calls=%fused_computation.112 | convolution fusion | flops 909639680 | bytes 4407552 | tf_op jit(solution)/shard_map/conv_general_dilated | solution.py:138
  163.7 9.0 %fusion.257 = f32[64,3,3,3,64]{0,4,3,2,1:T(8,128)} fusion(bf16[8,64,10,10,10]{1,0,4,3,2:T(8,128)(2,1)S(1)} %maximum_maximum_fusion.5, bf16[8,64,8,8,8]{1,0,4,3,2:T(8,128)(2,1)S(1)} %get-tuple-element.59), kind=kOutput, calls=%fused_computation.669 | convolution fusion | flops 905969664 | bytes 1990656 | tf_op jit(solution)/shard_map/transpose | solution.py:174
  174.4 3.2 copy.2861
  177.6 3.4 multiply_convert_fusion.2
  181.4 1.9 collective-permute-start.4
  185.6 2.2 copy.2859
  187.8 1.6 copy.2722
  189.5 2.6 collective-permute-start.5
  192.2 2.8 collective-permute-done.5
  228.8 6.2 %convert_reduce_fusion = (f32[64]{0:T(128)S(1)}, bf16[8,64,8,8,8]{1,0,4,3,2:T(8,128)(2,1)S(1)}, f32[8,64,8,8,8]{1,0,4,3,2:T(8,128)S(1)}) fusion(f32[8,64,8,8,8]{1,0,4,3,2:T(8,128)S(1)} %copy-done.24, f32[64]{0:T(128)S(1)} %copy-done.156, f32[8,8,8,8]{0,3,2,1:T(8,128)} %bitcast.759, bf16[64,3,3,3,64]{4,3,2,1,0:T(4,128)(2,1)S(1)} %copy-done.37, ...), kind=kOutput, calls=%fused_computation.108 | convolution fusion | flops 922951616 | bytes 3883520 | tf_op jit(solution)/shard_map/conv_general_dilated | solution.py:151
  235.0 7.9 %fusion.256 = f32[64,3,3,3,64]{0,4,3,2,1:T(8,128)S(1)} fusion(bf16[8,64,10,10,10]{1,0,4,3,2:T(8,128)(2,1)S(1)} %copy-done.26, bf16[8,64,8,8,8]{1,0,4,3,2:T(8,128)(2,1)S(1)} %get-tuple-element.43), kind=kOutput, calls=%fused_computation.668 | convolution fusion | flops 905969664 | bytes 1990656 | tf_op jit(solution)/shard_map/transpose | solution.py:174
  246.2 1.9 collective-permute-start.6
  249.3 2.4 collective-permute-start.7
  251.8 86.6 %all-reduce.34 = (f32[64]{0:T(128)}, f32[64]{0:T(128)}) all-reduce(f32[64]{0:T(128)S(1)} %get-tuple-element.42, f32[64]{0:T(128)S(1)} %copy-done.157), channel_id=1, replica_groups=mesh['bricks'=32,'scenes'=8] {'bricks','scenes'}, use_global_device_ids=true, to_apply=%region_3.4 | all-reduce | flops 128 | bytes 1024 | tf_op jit(solution)/shard_map/psum | solution.py:218
  372.2 5.5 %fusion.54 = f32[8,64,8,8,8]{1,0,4,3,2:T(8,128)} fusion(bf16[8,64,1,1,1]{1,0,4,3,2:T(8,128)(2,1)S(1)} %bitcast.829, bf16[8,64,1,1,8]{1,0,4,3,2:T(8,128)(2,1)S(1)} %bitcast.813, bf16[8,64,1,1,1]{1,0,4,3,2:T(8,128)(2,1)S(1)} %bitcast.831, bf16[8,64,1,8,1]{1,0,4,3,2:T(8,128)(2,1)S(1)} %bitcast.798, bf16[8,64,1,8,8]{1,0,4,3,2:T(8,128)(2,1)S(1)} %bitcast.765, ...), kind=kOutput, calls=%fused_computation.175 | convolution fusion | flops 919281664 | bytes 2293760 | tf_op jit(solution)/shard_map/conv_general_dilated | solution.py:151
  377.8 2.3 copy.2857
  380.2 1.7 multiply_convert_fusion.6
  381.9 132.4 %all-reduce.38.cloned.1.call-done = (f32[64,1728]{1,0:T(8,128)}, f32[64,1728]{1,0:T(8,128)}) async-done(((f32[64,1728]{1,0:T(8,128)}, f32[64,1728]{1,0:T(8,128)}), (f32[64,1728]{1,0:T(8,128)}, f32[64,1728]{1,0:T(8,128)})) %all-reduce.38.cloned.1.call-update) | async-done | bytes 884752 | tf_op jit(solution)/shard_map/psum | solution.py:218
  514.3 1.8 copy.3316
  516.1 1.8 copy.3317
  (724 shorter events, 172.0 us)
Async XLA Ops:
  7.2 507.1 %all-reduce.38.cloned.1.call-start = ((), (), s32[]{:S(2)}) async-start(), calls=%async_computation | async-start | bytes 1835008 | tf_op jit(solution)/shard_map/psum | solution.py:218
  11.5 19.4 %collective-permute-start.1 = (bf16[1,4,64,8,8]{2,1,4,3,0:T(4,128)(2,1)S(1)}, bf16[1,4,64,8,8]{2,1,4,3,0:T(4,128)(2,1)S(1)}, u32[]{:S(2)}, u32[]{:S(2)}) collective-permute-start(bf16[1,4,64,8,8]{2,1,4,3,0:T(4,128)(2,1)S(1)} %bitcast.788), channel_id=1, source_target_pairs={{8,0},{16,8},{24,16},{32,24},{40,32},{48,40},{56,48},{64,56},{72,6... | collective-permute-start | bytes 98312 | tf_op jit(solution)/shard_map/ppermute | solution.py:17
  16.7 14.0 %collective-permute-start = (bf16[1,4,64,8,8]{2,1,4,3,0:T(4,128)(2,1)S(1)}, bf16[1,4,64,8,8]{2,1,4,3,0:T(4,128)(2,1)S(1)}, u32[]{:S(2)}, u32[]{:S(2)}) collective-permute-start(bf16[1,4,64,8,8]{2,1,4,3,0:T(4,128)(2,1)S(1)} %bitcast.789), channel_id=1, source_target_pairs={{0,8},{8,16},{16,24},{24,32},{32,40},{40,48},{48,56},{56,64},{64,7... | collective-permute-start | bytes 98312 | tf_op jit(solution)/shard_map/ppermute | solution.py:16
  20.7 16.6 %copy-start.106 = (s32[8]{0:T(128)}, s32[8]{0:T(128)S(1)}, u32[]{:S(2)}) copy-start(s32[8]{0:T(128)S(1)} %get-tuple-element.17) | copy-start | bytes 100
  20.7 17.1 %copy-start.98 = (s32[8]{0:T(128)}, s32[8]{0:T(128)S(1)}, u32[]{:S(2)}) copy-start(s32[8]{0:T(128)S(1)} %get-tuple-element.18) | copy-start | bytes 100
  20.7 18.4 %copy-start.90 = (s32[8]{0:T(128)}, s32[8]{0:T(128)S(1)}, u32[]{:S(2)}) copy-start(s32[8]{0:T(128)S(1)} %get-tuple-element.19) | copy-start | bytes 100
  20.7 19.5 %copy-start.82 = (s32[8]{0:T(128)}, s32[8]{0:T(128)S(1)}, u32[]{:S(2)}) copy-start(s32[8]{0:T(128)S(1)} %get-tuple-element.20) | copy-start | bytes 100
  20.7 20.1 %copy-start.74 = (s32[8]{0:T(128)}, s32[8]{0:T(128)S(1)}, u32[]{:S(2)}) copy-start(s32[8]{0:T(128)S(1)} %get-tuple-element.21) | copy-start | bytes 100
  20.7 21.3 %copy-start.70 = (s32[8]{0:T(128)}, s32[8]{0:T(128)S(1)}, u32[]{:S(2)}) copy-start(s32[8]{0:T(128)S(1)} %get-tuple-element.22) | copy-start | bytes 100
  20.7 22.5 %copy-start.66 = (s32[8]{0:T(128)}, s32[8]{0:T(128)S(1)}, u32[]{:S(2)}) copy-start(s32[8]{0:T(128)S(1)} %get-tuple-element.23) | copy-start | bytes 100
  20.7 23.1 %copy-start.62 = (s32[8]{0:T(128)}, s32[8]{0:T(128)S(1)}, u32[]{:S(2)}) copy-start(s32[8]{0:T(128)S(1)} %get-tuple-element.24) | copy-start | bytes 100
  20.7 24.3 %copy-start.58 = (s32[8]{0:T(128)}, s32[8]{0:T(128)S(1)}, u32[]{:S(2)}) copy-start(s32[8]{0:T(128)S(1)} %get-tuple-element.25) | copy-start | bytes 100
  20.7 24.9 %copy-start.54 = (s32[8]{0:T(128)}, s32[8]{0:T(128)S(1)}, u32[]{:S(2)}) copy-start(s32[8]{0:T(128)S(1)} %get-tuple-element.26) | copy-start | bytes 100
  20.7 25.5 %copy-start.50 = (s32[8]{0:T(128)}, s32[8]{0:T(128)S(1)}, u32[]{:S(2)}) copy-start(s32[8]{0:T(128)S(1)} %get-tuple-element.27) | copy-start | bytes 100
  20.8 26.7 %copy-start.46 = (s32[8]{0:T(128)}, s32[8]{0:T(128)S(1)}, u32[]{:S(2)}) copy-start(s32[8]{0:T(128)S(1)} %get-tuple-element.28) | copy-start | bytes 100
  20.8 27.3 %copy-start.42 = (s32[8]{0:T(128)}, s32[8]{0:T(128)S(1)}, u32[]{:S(2)}) copy-start(s32[8]{0:T(128)S(1)} %get-tuple-element.29) | copy-start | bytes 100
  20.8 28.5 %copy-start.38 = (s32[8]{0:T(128)}, s32[8]{0:T(128)S(1)}, u32[]{:S(2)}) copy-start(s32[8]{0:T(128)S(1)} %get-tuple-element.30) | copy-start | bytes 100
  22.8 27.6 %copy-start.126 = (s32[8]{0:T(128)}, s32[8]{0:T(128)S(1)}, u32[]{:S(2)}) copy-start(s32[8]{0:T(128)S(1)} %get-tuple-element.32) | copy-start | bytes 100
  22.9 28.2 %copy-start.118 = (s32[8]{0:T(128)}, s32[8]{0:T(128)S(1)}, u32[]{:S(2)}) copy-start(s32[8]{0:T(128)S(1)} %get-tuple-element.33) | copy-start | bytes 100
  22.9 30.8 %copy-start.110 = (s32[8]{0:T(128)}, s32[8]{0:T(128)S(1)}, u32[]{:S(2)}) copy-start(s32[8]{0:T(128)S(1)} %get-tuple-element.34) | copy-start | bytes 100
  22.9 32.0 %copy-start.102 = (s32[8]{0:T(128)}, s32[8]{0:T(128)S(1)}, u32[]{:S(2)}) copy-start(s32[8]{0:T(128)S(1)} %get-tuple-element.35) | copy-start | bytes 100
  22.9 32.6 %copy-start.94 = (s32[8]{0:T(128)}, s32[8]{0:T(128)S(1)}, u32[]{:S(2)}) copy-start(s32[8]{0:T(128)S(1)} %get-tuple-element.36) | copy-start | bytes 100
  22.9 35.3 %copy-start.86 = (s32[8]{0:T(128)}, s32[8]{0:T(128)S(1)}, u32[]{:S(2)}) copy-start(s32[8]{0:T(128)S(1)} %get-tuple-element.37) | copy-start | bytes 100
  22.9 37.9 %copy-start.78 = (s32[8]{0:T(128)}, s32[8]{0:T(128)S(1)}, u32[]{:S(2)}) copy-start(s32[8]{0:T(128)S(1)} %get-tuple-element.31) | copy-start | bytes 100
  91.3 4.5 collective-permute-start.2
  93.4 5.6 %collective-permute-start.3 = (bf16[1,4,64,8,8]{2,1,4,3,0:T(4,128)(2,1)S(1)}, bf16[1,4,64,8,8]{2,1,4,3,0:T(4,128)(2,1)S(1)}, u32[]{:S(2)}, u32[]{:S(2)}) collective-permute-start(bf16[1,4,64,8,8]{2,1,4,3,0:T(4,128)(2,1)S(1)} %bitcast.793), channel_id=1, source_target_pairs={{8,0},{16,8},{24,16},{32,24},{40,32},{48,40},{56,48},{64,56},{72,6... | collective-permute-start | bytes 98312 | tf_op jit(solution)/shard_map/ppermute | solution.py:17
  128.4 16.4 %slice-start.1 = ((bf16[8,64,8,8]{1,3,2,0:T(8,128)(2,1)}), bf16[8,64,1,8]{1,3,2,0:T(8,128)(2,1)S(1)}, s32[]{:S(2)}) async-start(bf16[8,64,8,8]{1,3,2,0:T(8,128)(2,1)} %gather_fusion.27), calls=%async_computation.2 | async-start | bytes 32768 | tf_op jit(solution)/shard_map/slice | solution.py:68
  181.4 10.6 %collective-permute-start.4 = (bf16[1,4,64,8,8]{2,1,4,3,0:T(4,128)(2,1)S(1)}, bf16[1,4,64,8,8]{2,1,4,3,0:T(4,128)(2,1)S(1)}, u32[]{:S(2)}, u32[]{:S(2)}) collective-permute-start(bf16[1,4,64,8,8]{2,1,4,3,0:T(4,128)(2,1)S(1)} %bitcast.792), channel_id=1, source_target_pairs={{0,8},{8,16},{16,24},{24,32},{32,40},{40,48},{48,56},{56,64},{64,7... | collective-permute-start | bytes 98312 | tf_op jit(solution)/shard_map/ppermute | solution.py:16
  189.5 5.6 %collective-permute-start.5 = (bf16[1,4,64,8,8]{2,1,4,3,0:T(4,128)(2,1)S(1)}, bf16[1,4,64,8,8]{2,1,4,3,0:T(4,128)(2,1)S(1)}, u32[]{:S(2)}, u32[]{:S(2)}) collective-permute-start(bf16[1,4,64,8,8]{2,1,4,3,0:T(4,128)(2,1)S(1)} %bitcast.794), channel_id=1, source_target_pairs={{8,0},{16,8},{24,16},{32,24},{40,32},{48,40},{56,48},{64,56},{72,6... | collective-permute-start | bytes 98312 | tf_op jit(solution)/shard_map/ppermute | solution.py:17
  246.2 92.6 %copy-start.151 = (bf16[17]{0:T(256)(128)(2,1)S(1)}, bf16[17]{0:T(256)(128)(2,1)}, u32[]{:S(2)}) copy-start(bf16[17]{0:T(256)(128)(2,1)} %copy-done.148) | copy-start | bytes 106
  246.2 92.2 %collective-permute-start.6 = (bf16[1,4,64,8,8]{2,1,4,3,0:T(4,128)(2,1)S(1)}, bf16[1,4,64,8,8]{2,1,4,3,0:T(4,128)(2,1)S(1)}, u32[]{:S(2)}, u32[]{:S(2)}) collective-permute-start(bf16[1,4,64,8,8]{2,1,4,3,0:T(4,128)(2,1)S(1)} %bitcast.790), channel_id=1, source_target_pairs={{0,8},{8,16},{16,24},{24,32},{32,40},{40,48},{48,56},{56,64},{64,7... | collective-permute-start | bytes 98312 | tf_op jit(solution)/shard_map/ppermute | solution.py:16
  249.3 89.2 %collective-permute-start.7 = (bf16[1,4,64,8,8]{2,1,4,3,0:T(4,128)(2,1)S(1)}, bf16[1,4,64,8,8]{2,1,4,3,0:T(4,128)(2,1)S(1)}, u32[]{:S(2)}, u32[]{:S(2)}) collective-permute-start(bf16[1,4,64,8,8]{2,1,4,3,0:T(4,128)(2,1)S(1)} %bitcast.791), channel_id=1, source_target_pairs={{8,0},{16,8},{24,16},{32,24},{40,32},{48,40},{56,48},{64,56},{72,6... | collective-permute-start | bytes 98312 | tf_op jit(solution)/shard_map/ppermute | solution.py:17
  (148 other events, 609.5 us)
Sparse Core Ops, SparseCore 0:
  251.9 262.3 all-reduce.37
where the time goes:
time: 535 us; the launch traced here: 525 us
  local copies, waits for them, and re-layouts  179 us (33%)
  waiting for transfers between devices  138 us (26%)
  blocking collectives  86.6 us (16%)
  matrix products  46 us (9%)
  other arithmetic  37.9 us (7%)
  starting transfers between devices  20.2 us (4%)
  between operations  17.5 us (3%)
    psum x1, waiting for transfers between devices, local(): lax.psum((grad_weight_one, grad_weight_two, grad_bias_one, grad_bias_two)...  132 us
    gather x122, local copies, waits for them, and re-layouts, assemble(): face_rows = face_pool[lookup[:, number], face_number(offset)]  95.1 us
    psum x1, blocking collectives, local(): lax.psum((grad_weight_one, grad_weight_two, grad_bias_one, grad_bias_two)...  86.6 us
    slice x77, local copies, waits for them, and re-layouts, face_piece(): face_rows[:, :, cut_range(offset[1], edge_len), cut_range(offset[2], edge...  33.8 us
    concatenate x2, other arithmetic, assemble(): return jnp.concatenate(planes, axis=2)  19.8 us
    conv_general_dilated x2, matrix products, forward_conv(): lax.conv_general_dilated(padded, kernel_of(weight), (1, 1, 1), 'VALID', d...  17.3 us
    transpose x2, matrix products, weight_grad(): return result.transpose(1, 2, 3, 4, 0).reshape(channels, 27 * channels)  17 us
    unnamed x440, local copies, waits for them, and re-layouts  13.3 us
  transfers between devices with their start and end apart: 9, of which 3 were waited for; matrix products, arithmetic and copies ran while one was open for 12% of the time, Pallas kernels for 0%

commit v1 on v0

v1 whole, which is shorter than its diff:
```python
import functools

import jax
import jax.numpy as jnp
from jax import lax
from jax.experimental import pallas as pl
from jax.experimental.pallas import tpu as pltpu
from jax.sharding import PartitionSpec as P

C = 64
E = 8
S = 16
PL = S * S
L = 128
HALF = 512
BIAS_ROW = 864 - HALF
F32 = jnp.float32
BF16 = jnp.bfloat16


def dot_nn(a, b):
    return lax.dot_general(a, b, (((1,), (0,)), ((), ())), preferred_element_type=F32)


def dot_nt(a, b):
    return lax.dot_general(a, b, (((1,), (1,)), ((), ())), preferred_element_type=F32)


def eye(rows, cols):
    r = lax.broadcasted_iota(jnp.int32, (rows, cols), 0)
    c = lax.broadcasted_iota(jnp.int32, (rows, cols), 1)
    return jnp.where(r == c, 1.0, 0.0).astype(BF16)


def low_lanes(rows):
    return lax.broadcasted_iota(jnp.int32, (rows, L), 1) < C


def tap_of(dx, dy, dz):
    return 9 * (dx + 1) + 3 * (dy + 1) + (dz + 1)


def copy_to(src, dst, send, recv, device):
    return pltpu.make_async_remote_copy(
        src_ref=src,
        dst_ref=dst,
        send_sem=send,
        recv_sem=recv,
        device_id=device,
        device_id_type=pl.DeviceIdType.MESH,
    )


def sigmoid(v):
    return 1.0 / (1.0 + jnp.exp(-v))


def kernel(
    nb,
    ns,
    feat,
    cot,
    mask,
    w1,
    b1,
    w2,
    b2,
    out,
    gfeat,
    gw1,
    gw2,
    gb1,
    gb2,
    f0,
    f1,
    f2,
    yy,
    gt,
    u0,
    mm,
    ct,
    us,
    sl,
    gs,
    oo,
    wt,
    wd,
    wa,
    halo_out,
    halo_in,
    halo_wide,
    grads,
    pack,
    part1,
    sum1,
    part2,
    sum2,
    part3,
    sum3,
    full,
    halo_send,
    halo_recv,
    pair_send,
    pair_recv,
    chip_send,
    chip_recv,
    scene_send,
    scene_recv,
):
    nq = nb // 2
    b = lax.axis_index("bricks")
    s = lax.axis_index("scenes")
    core = lax.rem(b, 2)
    q = b // 2
    below = lax.rem(b + nb - 1, nb)
    above = lax.rem(b + 1, nb)
    other = b + 1 - 2 * core

    def chip_at(j):
        return {"bricks": 2 * lax.rem(q + j, nq) + core}

    def scene_at(j):
        return {"scenes": lax.rem(s + j, ns)}

    barrier = pltpu.get_barrier_semaphore()

    def greet(device):
        pl.semaphore_signal(barrier, inc=1, device_id=device, device_id_type=pl.DeviceIdType.MESH)

    greet({"bricks": below})
    greet({"bricks": above})
    lax.fori_loop(1, nq, lambda j, c: (greet(chip_at(j)), c)[1], 0)
    lax.fori_loop(1, ns, lambda j, c: (greet(scene_at(j)), c)[1], 0)

    eye256 = eye(PL, PL)
    eye128 = eye(L, L)
    eye64 = eye(C, C)
    eye64w = eye(C, L)

    def load_features(column, carry):
        bx, by = column // 2, lax.rem(column, 2)
        for bz in range(2):
            n = column * 2 + bz
            live = mask[0, pl.ds(n, 1), :].astype(F32)
            live = jnp.broadcast_to(live, (L, 2 * PL)).astype(BF16)
            masked = feat[0, n] * live[:C]
            for h in range(2):
                cols = slice(h * PL, (h + 1) * PL)
                stack = jnp.concatenate([masked[:, cols], masked[:, cols], live[:, cols]], axis=0)
                turned = dot_nt(eye256, stack)
                place = (pl.ds(bx * E + 4 * h, 4), pl.ds(by * E, E), slice(bz * E, bz * E + E))
                u0[place] = turned[:, :L].reshape(4, E, E, L)
                mm[place] = turned[:, L:].reshape(4, E, E, L)
        return carry

    def load_cotangent(column, carry):
        bx, by = column // 2, lax.rem(column, 2)
        for bz in range(2):
            value = cot[0, column * 2 + bz]
            for h in range(2):
                cols = slice(h * PL, (h + 1) * PL)
                stack = jnp.concatenate([value[:, cols], value[:, cols]], axis=0)
                place = (pl.ds(bx * E + 4 * h, 4), pl.ds(by * E, E), slice(bz * E, bz * E + E))
                ct[place] = dot_nt(eye256, stack).reshape(4, E, E, L)
        return carry

    def store_bricks(target):
        for n in range(8):
            bx, by, bz = n // 4, n // 2 % 2, n % 2
            rows = oo[bx * E : bx * E + E, by * E : by * E + E, bz * E : bz * E + E, :]
            rows = rows.reshape(E * E * E, L).astype(BF16)
            target[0, n] = dot_nt(eye64w, rows).astype(BF16)

    def prepare_weights(w, number, forward):
        spread = jnp.concatenate([eye64, eye64], axis=1)
        for m in range(14):
            size = L if m < 13 else C
            tile = w[:, m * L : m * L + size]
            if forward:
                twice = jnp.concatenate([tile, tile], axis=0)
                wt[m * L : m * L + size, :] = dot_nt(eye128 if m < 13 else eye64, twice)
            else:
                for part in range(size // C):
                    zeros = jnp.zeros((C, L), BF16)
                    if m == 13:
                        select = spread
                    else:
                        select = jnp.concatenate([spread, zeros] if part == 0 else [zeros, spread], axis=0)
                    k = 2 * m + part
                    wd[k * C : k * C + C, :] = dot_nn(tile, select)
        low = low_lanes(C)
        for dy in (-1, 0, 1):
            for i, dz in enumerate((-1, 0, 1)):

                def block(dx):
                    if forward:
                        k = tap_of(dx, dy, dz)
                        return wt[k * C : k * C + C, :]
                    k = tap_of(-dx, -dy, -dz)
                    return wd[k * C : k * C + C, :]

                rows = slice((dy + 1) * PL + i * C, (dy + 1) * PL + i * C + C)
                wa[number, rows, :L] = jnp.where(low, block(-1), block(1)).astype(BF16)
                wa[number, rows, L:] = block(0).astype(BF16)
            wa[number, (dy + 1) * PL + 3 * C : (dy + 2) * PL, :] = jnp.zeros((C, PL), BF16)

    low_half = low_lanes(PL // 2)

    def halo_copy(field, way):
        return copy_to(
            halo_out.at[field, way],
            halo_in.at[field, way],
            halo_send.at[field, way],
            halo_recv.at[field, way],
            {"bricks": above if way == 0 else below},
        )

    def send_halo(field):
        for way, z in ((0, S - 1), (1, 0)):
            plane = us[pl.ds(z, PL, stride=S), :]
            packed = jnp.where(low_half, plane[: PL // 2], plane[PL // 2 :])
            halo_out[field, way] = packed.astype(BF16)
            halo_copy(field, way).start()

    def receive_halo(field):
        for way in range(2):
            halo_copy(field, way).wait()
            got = halo_in[field, way].astype(F32)
            exists = (b > 0) if way == 0 else (b < nb - 1)
            got = got * jnp.where(exists, 1.0, 0.0)
            swapped = pltpu.roll(got, C, 1)
            halo_wide[way, : PL // 2, :] = jnp.where(low_half, got, swapped)
            halo_wide[way, PL // 2 :, :] = jnp.where(low_half, swapped, got)

    low_plane = low_lanes(PL)
    z_of = lax.broadcasted_iota(jnp.int32, (PL, L), 0) & (S - 1)

    def rows_of(x):
        return pl.ds(pl.multiple_of(x * PL, PL), PL)

    def fill(field):
        def step(x, carry):
            u = us[rows_of(x), :]
            at = pl.ds(pl.multiple_of(x * S, S), S)
            low_z = jnp.broadcast_to(halo_wide[0, at, :][:, None, :], (S, S, L)).reshape(PL, L)
            high_z = jnp.broadcast_to(halo_wide[1, at, :][:, None, :], (S, S, L)).reshape(PL, L)
            down = jnp.where(z_of == 0, low_z, pltpu.roll(u, 1, 0))
            up = jnp.where(z_of == S - 1, high_z, pltpu.roll(u, PL - 1, 0))
            tile = jnp.where(low_plane, down, u)
            field[x, 1 : S + 1, :, :L] = tile.reshape(S, S, L).astype(BF16)
            field[x, 1 : S + 1, :, L:] = up.reshape(S, S, L).astype(BF16)
            return carry

        lax.fori_loop(0, S, step, 0)

    def conv(field, number, first, last):
        def step(x, carry):
            rows = jnp.concatenate([field[x, e : e + S].reshape(PL, PL) for e in range(3)], axis=1)
            yy[x + 1] = dot_nn(rows, wa[number])
            return carry

        lax.fori_loop(first, last, step, 0)

    def conv_result(x):
        sides = jnp.where(low_plane, yy[x, :, :L], yy[x + 2, :, :L])
        return sides + pltpu.roll(sides, C, 1) + yy[x + 1, :, L:]

    def turn(x, value):
        gt[pl.ds(pl.multiple_of((x + 1) * C, C), C), :] = dot_nt(eye64w, value).astype(BF16)

    def weight_grad(field, number):
        grads[...] = jnp.zeros((3, 3 * C, PL), F32)

        def step(i, carry):
            left = jnp.concatenate(
                [gt[pl.ds(pl.multiple_of((4 * i + p) * C, C), 3 * C), :] for p in range(4)], axis=1
            )
            for e in range(3):
                right = field[pl.ds(4 * i, 4), e : e + S].reshape(4 * PL, PL)
                grads[e] += dot_nn(left, right)
            return carry

        lax.fori_loop(0, S // 4, step, 0)
        low = low_lanes(96)
        for e in range(3):
            for j in range(3):
                row = e * 3 * C + j * C
                pack[number, row // HALF, row % HALF : row % HALF + C, :] = grads[e, j * C : j * C + C, :L]
            row = 9 * C + e * 96 - HALF
            pack[number, 1, row : row + 96, :] = jnp.where(low, grads[e, :96, L:], grads[e, 96:, L:])

    def pack_bias(number, total):
        row = jnp.sum(total, axis=0, keepdims=True)
        pack[number, 1, BIAS_ROW : BIAS_ROW + 8, :] = jnp.broadcast_to(row, (8, L))

    def unpack(number, weight, bias):
        low = low_lanes(C)

        def piece(k):
            dx, dy, dz = k // 9, k // 3 % 3, k % 3
            j = 2 - dx
            if dz < 2:
                row = dy * 3 * C + j * C
                return packed(number, row, C), dz
            base = 9 * C + dy * 96
            if j == 0:
                return packed(number, base, C), 0
            if j == 2:
                return packed(number, base + 32, C), 1
            first = packed(number, base + 64, 32)
            second = pltpu.roll(packed(number, base, 32), C, 1)
            return jnp.concatenate([first, second], axis=0), 0

        def placed(k, half):
            value, at = piece(k)
            return value if at == half else pltpu.roll(value, C, 1)

        for m in range(13):
            weight[:, m * L : m * L + L] = jnp.where(low, placed(2 * m, 0), placed(2 * m + 1, 1))
        weight[:, 13 * L :] = placed(26, 0)[:, :C]
        bias[...] = full[number, 1, BIAS_ROW // chunk, BIAS_ROW % chunk : BIAS_ROW % chunk + 1, :C]

    chunk = HALF // nq

    def packed(number, row, size):
        half, at = row // HALF, row % HALF
        return full[number, half].reshape(HALF, L)[at : at + size]

    def pair_copy(number, step):
        if step == 0:
            src, dst = pack.at[number, 1 - core], part1.at[number]
        else:
            src, dst = full.at[number, core], full.at[number, core]
        return copy_to(src, dst, pair_send.at[number, step], pair_recv.at[number, step], {"bricks": other})

    def reduce_chips_copy(number, j):
        return copy_to(
            sum1.at[number, lax.rem(q + j, nq)],
            part2.at[number, j],
            chip_send.at[number, 0, j],
            chip_recv.at[number, 0, j],
            chip_at(j),
        )

    def scene_copy(number, j, sender):
        return copy_to(
            sum2.at[number],
            part3.at[number, sender],
            scene_send.at[number, j],
            scene_recv.at[number, j],
            scene_at(j),
        )

    def gather_chips_copy(number, j, sender):
        return copy_to(
            sum3.at[number],
            full.at[number, core, sender],
            chip_send.at[number, 1, j],
            chip_recv.at[number, 1, j],
            chip_at(j),
        )

    def each(count, act):
        def step(j, carry):
            act(j)
            return carry

        lax.fori_loop(1, count, step, 0)

    def sum_start(number):
        pair_copy(number, 0).start()

    def sum_chips(number):
        pair_copy(number, 0).wait()
        total = pack[number, core] + part1[number]
        sum1[number] = total.reshape(nq, chunk, L)
        each(nq, lambda j: reduce_chips_copy(number, j).start())

    def sum_scenes(number):
        each(nq, lambda j: reduce_chips_copy(number, j).wait())
        total = sum1[number, q]
        for j in range(1, nq):
            total += part2[number, j]
        sum2[number] = total
        part3[number, s] = total
        each(ns, lambda j: scene_copy(number, j, s).start())

    def gather_chips(number):
        each(ns, lambda j: scene_copy(number, j, lax.rem(s + ns - j, ns)).wait())
        total = part3[number, 0]
        for j in range(1, ns):
            total += part3[number, j]
        sum3[number] = total
        full[number, core, q] = total
        each(nq, lambda j: gather_chips_copy(number, j, q).start())

    def gather_pair(number):
        each(nq, lambda j: gather_chips_copy(number, j, lax.rem(q + nq - j, nq)).wait())
        pair_copy(number, 1).start()

    def sum_end(number):
        pair_copy(number, 1).wait()

    for field in (f0, f1, f2):
        field[:, 0] = jnp.zeros((S, S, PL), BF16)
        field[:, S + 1] = jnp.zeros((S, S, PL), BF16)
    yy[0] = jnp.zeros((PL, PL), F32)
    yy[S + 1] = jnp.zeros((PL, PL), F32)
    gt[:C] = jnp.zeros((C, PL), BF16)
    gt[(S + 1) * C :] = jnp.zeros((C, PL), BF16)
    for number in range(2):
        pack[number, 1, BIAS_ROW:, :] = jnp.zeros((HALF - BIAS_ROW, L), F32)

    lax.fori_loop(0, 4, load_features, 0)

    def copy_in(x, carry):
        us[rows_of(x), :] = u0[x].reshape(PL, L)
        return carry

    lax.fori_loop(0, S, copy_in, 0)
    pl.semaphore_wait(barrier, 2 + (nq - 1) + (ns - 1))
    send_halo(0)
    prepare_weights(w1, 0, True)
    receive_halo(0)
    fill(f0)
    conv(f0, 0, 0, S)

    def after_first(x, carry):
        live = mm[x].reshape(PL, L)
        bias = jnp.concatenate([b1[...], b1[...]], axis=1)
        first = live * (conv_result(x) + bias)
        sig = sigmoid(first)
        hidden = first * sig
        sl[rows_of(x), :] = live * (sig + hidden * (1.0 - sig))
        us[rows_of(x), :] = hidden.astype(BF16).astype(F32)
        return carry

    lax.fori_loop(0, S, after_first, 0)
    send_halo(1)
    prepare_weights(w2, 1, True)
    prepare_weights(w2, 2, False)
    prepare_weights(w1, 3, False)
    lax.fori_loop(0, 4, load_cotangent, 0)
    receive_halo(1)
    fill(f1)
    conv(f1, 1, 0, S)

    def after_second(x, carry):
        live = mm[x].reshape(PL, L)
        bias = jnp.concatenate([b2[...], b2[...]], axis=1)
        summed = live * (conv_result(x) + bias) + u0[x].reshape(PL, L)
        sig = sigmoid(summed)
        value = summed * sig
        oo[x] = value.reshape(S, S, L)
        slope = sig + value * (1.0 - sig)
        grad = (ct[x].reshape(PL, L) * slope * live).astype(BF16)
        turn(x, grad)
        grad = grad.astype(F32)
        us[rows_of(x), :] = grad
        gs[rows_of(x), :] = grad
        return carry + jnp.sum(grad.reshape(PL // 8, 8, L), axis=0)

    total = lax.fori_loop(0, S, after_second, jnp.zeros((8, L), F32))
    send_halo(2)
    pack_bias(1, total)
    weight_grad(f1, 1)
    sum_start(1)
    store_bricks(out)
    receive_halo(2)
    fill(f2)
    sum_chips(1)
    conv(f2, 2, 0, S)
    sum_scenes(1)

    def after_third(x, carry):
        grad = (conv_result(x) * sl[rows_of(x), :]).astype(BF16)
        turn(x, grad)
        grad = grad.astype(F32)
        us[rows_of(x), :] = grad
        return carry + jnp.sum(grad.reshape(PL // 8, 8, L), axis=0)

    total = lax.fori_loop(0, S, after_third, jnp.zeros((8, L), F32))
    send_halo(3)
    gather_chips(1)
    pack_bias(0, total)
    weight_grad(f0, 0)
    sum_start(0)
    gather_pair(1)
    receive_halo(3)
    fill(f2)
    sum_chips(0)
    conv(f2, 3, 0, S)
    sum_scenes(0)
    sum_end(1)

    def after_fourth(x, carry):
        value = mm[x].reshape(PL, L) * (gs[rows_of(x), :] + conv_result(x))
        oo[x] = value.reshape(S, S, L)
        return carry

    lax.fori_loop(0, S, after_fourth, 0)
    gather_chips(0)
    store_bricks(gfeat)
    gather_pair(0)
    unpack(1, gw2, gb2)
    sum_end(0)
    unpack(0, gw1, gb1)


def local(nb, ns, features, cotangent, mask, w1, b1, w2, b2):
    nq = nb // 2
    chunk = HALF // nq
    vmem = pltpu.VMEM
    field = vmem((S, S + 2, S, PL), BF16)
    block4 = vmem((S, S, S, L), F32)
    block2 = vmem((S * PL, L), F32)
    dma = pltpu.SemaphoreType.DMA
    scratch = [
        field,
        field,
        field,
        vmem((S + 2, PL, PL), F32),
        vmem(((S + 2) * C, PL), BF16),
        block4,
        block4,
        block4,
        block2,
        block2,
        block2,
        block4,
        vmem((27 * C, L), F32),
        vmem((27 * C, L), F32),
        vmem((4, 3 * PL, PL), BF16),
        vmem((4, 2, PL // 2, L), BF16),
        vmem((4, 2, PL // 2, L), BF16),
        vmem((2, PL, L), F32),
        vmem((3, 3 * C, PL), F32),
        vmem((2, 2, HALF, L), F32),
        vmem((2, HALF, L), F32),
        vmem((2, nq, chunk, L), F32),
        vmem((2, nq, chunk, L), F32),
        vmem((2, chunk, L), F32),
        vmem((2, ns, chunk, L), F32),
        vmem((2, chunk, L), F32),
        vmem((2, 2, nq, chunk, L), F32),
        dma((4, 2)),
        dma((4, 2)),
        dma((2, 2)),
        dma((2, 2)),
        dma((2, 2, nq)),
        dma((2, 2, nq)),
        dma((2, ns)),
        dma((2, ns)),
    ]
    shape = jax.ShapeDtypeStruct
    in_vmem = pl.BlockSpec(memory_space=pltpu.VMEM)
    output, grad_features, gw1, gw2, gb1, gb2 = pl.pallas_call(
        functools.partial(kernel, nb, ns),
        out_shape=[
            shape(features.shape, BF16),
            shape(features.shape, BF16),
            shape(w1.shape, F32),
            shape(w2.shape, F32),
            shape((1, C), F32),
            shape((1, C), F32),
        ],
        in_specs=[in_vmem] * 7,
        out_specs=[in_vmem] * 6,
        scratch_shapes=scratch,
        compiler_params=pltpu.CompilerParams(
            collective_id=0, has_side_effects=True, vmem_limit_bytes=56 * 1024 * 1024
        ),
        name="residual_block",
    )(features, cotangent, mask, w1, b1.reshape(1, C), w2, b2.reshape(1, C))
    return output, grad_features, gw1, gw2, gb1.reshape(C), gb2.reshape(C)


def solution(mesh):
    nb, ns = mesh.shape["bricks"], mesh.shape["scenes"]

    def program(features, cotangent, neighbours, mask, weight_one, bias_one, weight_two, bias_two):
        del neighbours
        split = P("scenes", "bricks", None, None)
        return jax.shard_map(
            functools.partial(local, nb, ns),
            mesh=mesh,
            in_specs=(split, split, P("scenes", "bricks", None), P(), P(), P(), P()),
            out_specs=(split, split, P(), P(), P(), P()),
            check_vma=False,
        )(features, cotangent, mask, weight_one, bias_one, weight_two, bias_two)

    return program
```

time: 535 us -> 89.8 us (0.17); the launches traced: 525 us -> 89.6 us
  local copies, waits for them, and re-layouts: 179 us -> 6.2 us
  waiting for transfers between devices: 138 us -> 0 us
  blocking collectives: 86.6 us -> 0 us
  Pallas kernels: 0 us -> 82.8 us
  matrix products: 46 us -> 0 us
  other arithmetic: 37.9 us -> 0 us
  starting transfers between devices: 20.2 us -> 0 us
  between operations: 17.5 us -> 0.66 us
    psum x1 -> x0, waiting for transfers between devices: 132 us -> none  [local(): lax.psum((grad_weight_one, grad_weight_two, grad_bias_one, grad_bias_two)...]
    gather x122 -> x0, local copies, waits for them, and re-layouts: 95.1 us -> none  [assemble(): face_rows = face_pool[lookup[:, number], face_number(offset)]]
    psum x1 -> x0, blocking collectives: 86.6 us -> none  [local(): lax.psum((grad_weight_one, grad_weight_two, grad_bias_one, grad_bias_two)...]
    pallas_call x0 -> x1, Pallas kernels: none -> 82.8 us  [local(): pl.pallas_call(functools.partial(kernel, nb, ns), out_shape=[shape(featur...]
    slice x97 -> x0, local copies, waits for them, and re-layouts: 41.1 us -> none  [the longest x77 33.8 us: face_piece(): face_rows[:, :, cut_range(offset[1], edge_len), cut_range(offset[2], edge...]
    conv_general_dilated x4 -> x0, matrix products: 29 us -> none  [the longest x2 17.3 us: forward_conv(): lax.conv_general_dilated(padded, kernel_of(weight), (1, 1, 1), 'VALID', d...]
    concatenate x8 -> x0, other arithmetic: 26.8 us -> none  [the longest x2 19.8 us: assemble(): return jnp.concatenate(planes, axis=2)]
    ppermute x8 -> x0, starting transfers between devices: 20.2 us -> none  [the longest x4 12.5 us: padded_2(): after = lax.ppermute(first, axis, down)]
  transfers between devices with their start and end apart: 9 -> 0, of which waited for: 3 -> 0; matrix products, arithmetic and copies ran while one was open for 12% -> 0% of each run, Pallas kernels for 0% -> 0%
where the time goes in v1:
time: 89.8 us; the launch traced here: 89.6 us
  Pallas kernels  82.8 us (92%)
  local copies, waits for them, and re-layouts  6.2 us (7%)
    pallas_call x1, Pallas kernels, local(): pl.pallas_call(functools.partial(kernel, nb, ns), out_shape=[shape(featur...  82.8 us
    unnamed x16, local copies, waits for them, and re-layouts  6.2 us

profile of v1, /device:TPU:1, one launch (start us, length us, event | category | flops | bytes accessed | tf_op | source)
XLA Modules:
  0.0 89.6 jit_solution(2149397293655579664)
XLA Ops:
  0.6 82.8 %residual_block.1 = (bf16[1,8,64,512]{3,2,1,0:T(8,128)(2,1)}, bf16[1,8,64,512]{3,2,1,0:T(8,128)(2,1)}, f32[64,1728]{1,0:T(8,128)}, f32[64,1728]{1,0:T(8,128)}, f32[1,64]{1,0:T(1,128)}, /*index=5*/f32[1,64]{1,0:T(1,128)}) custom-call(bf16[1,8,64,512]{3,2,1,0:T(8,128)(2,1)} %feat.1, bf16[1,8,64,512]{3,2,1,0:T(8,128)(2,1)} %cot.1, s32[1,8,512]{2,1,0:T(8,128)} %mask.1, ...), custom_call_target="tpu_custom_call" | custom-call | tf_op jit(solution)/shard_map/residual_block/pallas_call | solution.py:557
  83.4 0.0 copy-start
  83.4 1.9 %copy.19 = bf16[1,8,64,512]{3,2,1,0:T(8,128)(2,1)} copy(bf16[1,8,64,512]{3,2,1,0:T(8,128)(2,1)} %get-tuple-element.24) | data formatting | bytes 1048576
  85.3 0.0 copy-done
  85.3 0.0 copy-start.2
  85.3 0.8 copy.20
  86.1 0.4 copy-done.2
  86.5 0.0 copy-start.1
  86.5 0.8 copy.21
  87.3 0.4 copy-done.1
  87.7 0.0 copy-start.4
  87.7 0.8 copy.22
  88.5 0.0 copy-done.4
  88.5 0.0 copy-start.3
  88.5 0.5 copy.23
  89.0 0.1 copy-done.3
  89.1 0.5 copy.24
Async XLA Ops:
  83.4 1.9 %copy-start = (bf16[1,8,64,512]{3,2,1,0:T(8,128)(2,1)S(1)}, bf16[1,8,64,512]{3,2,1,0:T(8,128)(2,1)}, u32[]{:S(2)}) copy-start(bf16[1,8,64,512]{3,2,1,0:T(8,128)(2,1)} %get-tuple-element.25) | copy-start | bytes 1572868
  85.3 1.2 %copy-start.2 = (f32[64,1728]{1,0:T(8,128)S(1)}, f32[64,1728]{1,0:T(8,128)}, u32[]{:S(2)}) copy-start(f32[64,1728]{1,0:T(8,128)} %get-tuple-element.26) | copy-start | bytes 1327108
  86.5 1.2 %copy-start.1 = (f32[64,1728]{1,0:T(8,128)S(1)}, f32[64,1728]{1,0:T(8,128)}, u32[]{:S(2)}) copy-start(f32[64,1728]{1,0:T(8,128)} %get-tuple-element.27) | copy-start | bytes 1327108
  87.7 0.8 copy-start.4
  88.5 0.6 copy-start.3

commit v2 on v1

--- a/solution.py
+++ b/solution.py
@@ -59,18 +59,17 @@
     nb,
     ns,
     feat,
-    cot,
+    cot_hbm,
     mask,
     w1,
     b1,
-    w2,
+    w2_hbm,
     b2,
     out,
     gfeat,
-    gw1,
-    gw2,
-    gb1,
-    gb2,
+    sums,
+    cot,
+    w2,
     f0,
     f1,
     f2,
@@ -83,6 +82,7 @@
     sl,
     gs,
     oo,
+    o2,
     wt,
     wd,
     wa,
@@ -106,6 +106,7 @@
     chip_recv,
     scene_send,
     scene_recv,
+    load_sem,
 ):
     nq = nb // 2
     b = lax.axis_index("bricks")
@@ -122,6 +123,11 @@
     def scene_at(j):
         return {"scenes": lax.rem(s + j, ns)}
 
+    cot_load = pltpu.make_async_copy(cot_hbm, cot, load_sem.at[0])
+    w2_load = pltpu.make_async_copy(w2_hbm, w2, load_sem.at[1])
+    cot_load.start()
+    w2_load.start()
+
     barrier = pltpu.get_barrier_semaphore()
 
     def greet(device):
@@ -129,42 +135,44 @@
 
     greet({"bricks": below})
     greet({"bricks": above})
-    lax.fori_loop(1, nq, lambda j, c: (greet(chip_at(j)), c)[1], 0)
-    lax.fori_loop(1, ns, lambda j, c: (greet(scene_at(j)), c)[1], 0)
+    for j in range(1, nq):
+        greet(chip_at(j))
+    for j in range(1, ns):
+        greet(scene_at(j))
 
     eye256 = eye(PL, PL)
     eye128 = eye(L, L)
     eye64 = eye(C, C)
     eye64w = eye(C, L)
 
-    def load_features(column, carry):
-        bx, by = column // 2, lax.rem(column, 2)
+    def load_features(column):
+        bx, by = column // 2, column % 2
         for bz in range(2):
             n = column * 2 + bz
-            live = mask[0, pl.ds(n, 1), :].astype(F32)
+            live = mask[0, n : n + 1, :].astype(F32)
             live = jnp.broadcast_to(live, (L, 2 * PL)).astype(BF16)
             masked = feat[0, n] * live[:C]
             for h in range(2):
                 cols = slice(h * PL, (h + 1) * PL)
                 stack = jnp.concatenate([masked[:, cols], masked[:, cols], live[:, cols]], axis=0)
                 turned = dot_nt(eye256, stack)
-                place = (pl.ds(bx * E + 4 * h, 4), pl.ds(by * E, E), slice(bz * E, bz * E + E))
+                x, y, z = bx * E + 4 * h, by * E, bz * E
+                place = (slice(x, x + 4), slice(y, y + E), slice(z, z + E))
                 u0[place] = turned[:, :L].reshape(4, E, E, L)
                 mm[place] = turned[:, L:].reshape(4, E, E, L)
-        return carry
-
-    def load_cotangent(column, carry):
-        bx, by = column // 2, lax.rem(column, 2)
+
+    def load_cotangent(column):
+        bx, by = column // 2, column % 2
         for bz in range(2):
             value = cot[0, column * 2 + bz]
             for h in range(2):
                 cols = slice(h * PL, (h + 1) * PL)
                 stack = jnp.concatenate([value[:, cols], value[:, cols]], axis=0)
-                place = (pl.ds(bx * E + 4 * h, 4), pl.ds(by * E, E), slice(bz * E, bz * E + E))
+                x, y, z = bx * E + 4 * h, by * E, bz * E
+                place = (slice(x, x + 4), slice(y, y + E), slice(z, z + E))
                 ct[place] = dot_nt(eye256, stack).reshape(4, E, E, L)
-        return carry
-
-    def store_bricks(target):
+
+    def store_bricks(oo, target):
         for n in range(8):
             bx, by, bz = n // 4, n // 2 % 2, n % 2
             rows = oo[bx * E : bx * E + E, by * E : by * E + E, bz * E : bz * E + E, :]
@@ -224,7 +232,7 @@
 
     def receive_halo(field):
         for way in range(2):
-            halo_copy(field, way).wait()
+            halo_copy(field, way).wait_recv()
             got = halo_in[field, way].astype(F32)
             exists = (b > 0) if way == 0 else (b < nb - 1)
             got = got * jnp.where(exists, 1.0, 0.0)
@@ -236,12 +244,12 @@
     z_of = lax.broadcasted_iota(jnp.int32, (PL, L), 0) & (S - 1)
 
     def rows_of(x):
-        return pl.ds(pl.multiple_of(x * PL, PL), PL)
+        return slice(x * PL, x * PL + PL)
 
     def fill(field):
-        def step(x, carry):
+        for x in range(S):
             u = us[rows_of(x), :]
-            at = pl.ds(pl.multiple_of(x * S, S), S)
+            at = slice(x * S, x * S + S)
             low_z = jnp.broadcast_to(halo_wide[0, at, :][:, None, :], (S, S, L)).reshape(PL, L)
             high_z = jnp.broadcast_to(halo_wide[1, at, :][:, None, :], (S, S, L)).reshape(PL, L)
             down = jnp.where(z_of == 0, low_z, pltpu.roll(u, 1, 0))
@@ -249,38 +257,22 @@
             tile = jnp.where(low_plane, down, u)
             field[x, 1 : S + 1, :, :L] = tile.reshape(S, S, L).astype(BF16)
             field[x, 1 : S + 1, :, L:] = up.reshape(S, S, L).astype(BF16)
-            return carry
-
-        lax.fori_loop(0, S, step, 0)
-
-    def conv(field, number, first, last):
-        def step(x, carry):
-            rows = jnp.concatenate([field[x, e : e + S].reshape(PL, PL) for e in range(3)], axis=1)
-            yy[x + 1] = dot_nn(rows, wa[number])
-            return carry
-
-        lax.fori_loop(first, last, step, 0)
+
+    def conv(field, number):
+        rows = jnp.concatenate([field[:, e : e + S].reshape(S * PL, PL) for e in range(3)], axis=1)
+        yy[1 : S + 1] = dot_nn(rows, wa[number]).reshape(S, PL, PL)
 
     def conv_result(x):
         sides = jnp.where(low_plane, yy[x, :, :L], yy[x + 2, :, :L])
         return sides + pltpu.roll(sides, C, 1) + yy[x + 1, :, L:]
 
     def turn(x, value):
-        gt[pl.ds(pl.multiple_of((x + 1) * C, C), C), :] = dot_nt(eye64w, value).astype(BF16)
+        gt[(x + 1) * C : (x + 2) * C, :] = dot_nt(eye64w, value).astype(BF16)
 
     def weight_grad(field, number):
-        grads[...] = jnp.zeros((3, 3 * C, PL), F32)
-
-        def step(i, carry):
-            left = jnp.concatenate(
-                [gt[pl.ds(pl.multiple_of((4 * i + p) * C, C), 3 * C), :] for p in range(4)], axis=1
-            )
-            for e in range(3):
-                right = field[pl.ds(4 * i, 4), e : e + S].reshape(4 * PL, PL)
-                grads[e] += dot_nn(left, right)
-            return carry
-
-        lax.fori_loop(0, S // 4, step, 0)
+        left = jnp.concatenate([gt[x * C : (x + 3) * C, :] for x in range(S)], axis=1)
+        for e in range(3):
+            grads[e] = dot_nn(left, field[:, e : e + S].reshape(S * PL, PL))
         low = low_lanes(96)
         for e in range(3):
             for j in range(3):
@@ -291,40 +283,17 @@
 
     def pack_bias(number, total):
         row = jnp.sum(total, axis=0, keepdims=True)
-        pack[number, 1, BIAS_ROW : BIAS_ROW + 8, :] = jnp.broadcast_to(row, (8, L))
-
-    def unpack(number, weight, bias):
-        low = low_lanes(C)
-
-        def piece(k):
-            dx, dy, dz = k // 9, k // 3 % 3, k % 3
-            j = 2 - dx
-            if dz < 2:
-                row = dy * 3 * C + j * C
-                return packed(number, row, C), dz
-            base = 9 * C + dy * 96
-            if j == 0:
-                return packed(number, base, C), 0
-            if j == 2:
-                return packed(number, base + 32, C), 1
-            first = packed(number, base + 64, 32)
-            second = pltpu.roll(packed(number, base, 32), C, 1)
-            return jnp.concatenate([first, second], axis=0), 0
-
-        def placed(k, half):
-            value, at = piece(k)
-            return value if at == half else pltpu.roll(value, C, 1)
-
-        for m in range(13):
-            weight[:, m * L : m * L + L] = jnp.where(low, placed(2 * m, 0), placed(2 * m + 1, 1))
-        weight[:, 13 * L :] = placed(26, 0)[:, :C]
-        bias[...] = full[number, 1, BIAS_ROW // chunk, BIAS_ROW % chunk : BIAS_ROW % chunk + 1, :C]
+        pack[number, 1, BIAS_ROW : BIAS_ROW + 1, :] = row
 
     chunk = HALF // nq
 
-    def packed(number, row, size):
-        half, at = row // HALF, row % HALF
-        return full[number, half].reshape(HALF, L)[at : at + size]
+    def split_bias(value, first_row):
+        row = lax.broadcasted_iota(jnp.int32, value.shape, 0) + first_row
+        at = BIAS_ROW % chunk if value.shape[0] == chunk else BIAS_ROW
+        whole = value[at : at + 1] + value[at + 1 : at + 2]
+        high = whole.astype(BF16).astype(F32)
+        value = jnp.where(row == HALF + BIAS_ROW, high, value)
+        return jnp.where(row == HALF + BIAS_ROW + 1, whole - high, value)
 
     def pair_copy(number, step):
         if step == 0:
@@ -360,46 +329,56 @@
             chip_at(j),
         )
 
-    def each(count, act):
-        def step(j, carry):
-            act(j)
-            return carry
-
-        lax.fori_loop(1, count, step, 0)
-
     def sum_start(number):
         pair_copy(number, 0).start()
 
     def sum_chips(number):
-        pair_copy(number, 0).wait()
-        total = pack[number, core] + part1[number]
-        sum1[number] = total.reshape(nq, chunk, L)
-        each(nq, lambda j: reduce_chips_copy(number, j).start())
+        pair_copy(number, 0).wait_recv()
+        total = split_bias(pack[number, core] + part1[number], core * HALF)
+        sum1[number] = total.astype(BF16).reshape(nq, chunk, L)
+        for j in range(1, nq):
+            reduce_chips_copy(number, j).start()
 
     def sum_scenes(number):
-        each(nq, lambda j: reduce_chips_copy(number, j).wait())
-        total = sum1[number, q]
         for j in range(1, nq):
-            total += part2[number, j]
+            reduce_chips_copy(number, j).wait_recv()
+        total = sum1[number, q].astype(F32)
+        for j in range(1, nq):
+            total += part2[number, j].astype(F32)
+        total = split_bias(total, core * HALF + q * chunk).astype(BF16)
         sum2[number] = total
         part3[number, s] = total
-        each(ns, lambda j: scene_copy(number, j, s).start())
+        for j in range(1, ns):
+            scene_copy(number, j, s).start()
 
     def gather_chips(number):
-        each(ns, lambda j: scene_copy(number, j, lax.rem(s + ns - j, ns)).wait())
-        total = part3[number, 0]
         for j in range(1, ns):
-            total += part3[number, j]
+            scene_copy(number, j, lax.rem(s + ns - j, ns)).wait_recv()
+        total = part3[number, 0].astype(F32)
+        for j in range(1, ns):
+            total += part3[number, j].astype(F32)
+        total = split_bias(total, core * HALF + q * chunk).astype(BF16)
         sum3[number] = total
         full[number, core, q] = total
-        each(nq, lambda j: gather_chips_copy(number, j, q).start())
+        for j in range(1, nq):
+            gather_chips_copy(number, j, q).start()
 
     def gather_pair(number):
-        each(nq, lambda j: gather_chips_copy(number, j, lax.rem(q + nq - j, nq)).wait())
+        for j in range(1, nq):
+            gather_chips_copy(number, j, lax.rem(q + nq - j, nq)).wait_recv()
         pair_copy(number, 1).start()
 
     def sum_end(number):
-        pair_copy(number, 1).wait()
+        pair_copy(number, 1).wait_recv()
+
+    def sends_end(number):
+        pair_copy(number, 0).wait_send()
+        pair_copy(number, 1).wait_send()
+        for j in range(1, nq):
+            reduce_chips_copy(number, j).wait_send()
+            gather_chips_copy(number, j, q).wait_send()
+        for j in range(1, ns):
+            scene_copy(number, j, s).wait_send()
 
     for field in (f0, f1, f2):
         field[:, 0] = jnp.zeros((S, S, PL), BF16)
@@ -411,21 +390,18 @@
     for number in range(2):
         pack[number, 1, BIAS_ROW:, :] = jnp.zeros((HALF - BIAS_ROW, L), F32)
 
-    lax.fori_loop(0, 4, load_features, 0)
-
-    def copy_in(x, carry):
+    for column in range(4):
+        load_features(column)
+    for x in range(S):
         us[rows_of(x), :] = u0[x].reshape(PL, L)
-        return carry
-
-    lax.fori_loop(0, S, copy_in, 0)
     pl.semaphore_wait(barrier, 2 + (nq - 1) + (ns - 1))
     send_halo(0)
     prepare_weights(w1, 0, True)
     receive_halo(0)
     fill(f0)
-    conv(f0, 0, 0, S)
-
-    def after_first(x, carry):
+    conv(f0, 0)
+
+    def after_first(x):
         live = mm[x].reshape(PL, L)
         bias = jnp.concatenate([b1[...], b1[...]], axis=1)
         first = live * (conv_result(x) + bias)
@@ -433,19 +409,22 @@
         hidden = first * sig
         sl[rows_of(x), :] = live * (sig + hidden * (1.0 - sig))
         us[rows_of(x), :] = hidden.astype(BF16).astype(F32)
-        return carry
-
-    lax.fori_loop(0, S, after_first, 0)
+
+    for x in range(S):
+        after_first(x)
     send_halo(1)
+    w2_load.wait()
     prepare_weights(w2, 1, True)
     prepare_weights(w2, 2, False)
     prepare_weights(w1, 3, False)
-    lax.fori_loop(0, 4, load_cotangent, 0)
+    cot_load.wait()
+    for column in range(4):
+        load_cotangent(column)
     receive_halo(1)
     fill(f1)
-    conv(f1, 1, 0, S)
-
-    def after_second(x, carry):
+    conv(f1, 1)
+
+    def after_second(x):
         live = mm[x].reshape(PL, L)
         bias = jnp.concatenate([b2[...], b2[...]], axis=1)
         summed = live * (conv_result(x) + bias) + u0[x].reshape(PL, L)
@@ -458,53 +437,100 @@
         grad = grad.astype(F32)
         us[rows_of(x), :] = grad
         gs[rows_of(x), :] = grad
-        return carry + jnp.sum(grad.reshape(PL // 8, 8, L), axis=0)
-
-    total = lax.fori_loop(0, S, after_second, jnp.zeros((8, L), F32))
+        return jnp.sum(grad.reshape(PL // 8, 8, L), axis=0)
+
+    total = jnp.zeros((8, L), F32)
+    for x in range(S):
+        total += after_second(x)
     send_halo(2)
     pack_bias(1, total)
     weight_grad(f1, 1)
     sum_start(1)
-    store_bricks(out)
     receive_halo(2)
     fill(f2)
+    conv(f2, 2)
     sum_chips(1)
-    conv(f2, 2, 0, S)
-    sum_scenes(1)
-
-    def after_third(x, carry):
+
+    def after_third(x):
         grad = (conv_result(x) * sl[rows_of(x), :]).astype(BF16)
         turn(x, grad)
         grad = grad.astype(F32)
         us[rows_of(x), :] = grad
-        return carry + jnp.sum(grad.reshape(PL // 8, 8, L), axis=0)
-
-    total = lax.fori_loop(0, S, after_third, jnp.zeros((8, L), F32))
+        return jnp.sum(grad.reshape(PL // 8, 8, L), axis=0)
+
+    total = jnp.zeros((8, L), F32)
+    for x in range(S):
+        total += after_third(x)
     send_halo(3)
-    gather_chips(1)
     pack_bias(0, total)
     weight_grad(f0, 0)
     sum_start(0)
-    gather_pair(1)
+    sum_scenes(1)
+    sum_chips(0)
     receive_halo(3)
     fill(f2)
-    sum_chips(0)
-    conv(f2, 3, 0, S)
+    conv(f2, 3)
+
+    def after_fourth(x):
+        value = mm[x].reshape(PL, L) * (gs[rows_of(x), :] + conv_result(x))
+        o2[x] = value.reshape(S, S, L)
+
+    gather_chips(1)
+    store_bricks(oo, out)
     sum_scenes(0)
+    for x in range(S):
+        after_fourth(x)
+    gather_pair(1)
+    gather_chips(0)
+    store_bricks(o2, gfeat)
     sum_end(1)
-
-    def after_fourth(x, carry):
-        value = mm[x].reshape(PL, L) * (gs[rows_of(x), :] + conv_result(x))
-        oo[x] = value.reshape(S, S, L)
-        return carry
-
-    lax.fori_loop(0, S, after_fourth, 0)
-    gather_chips(0)
-    store_bricks(gfeat)
+    sums[1] = full[1].reshape(2, HALF, L)
     gather_pair(0)
-    unpack(1, gw2, gb2)
+    sends_end(1)
     sum_end(0)
-    unpack(0, gw1, gb1)
+    sums[0] = full[0].reshape(2, HALF, L)
+    sends_end(0)
+    for field in range(4):
+        for way in range(2):
+            halo_copy(field, way).wait_send()
+
+
+def unpack(sums, number, weight, bias):
+    low = low_lanes(C)
+
+    def packed(row, size):
+        return sums[number, row // HALF, row % HALF : row % HALF + size, :].astype(F32)
+
+    def piece(k):
+        dx, dy, dz = k // 9, k // 3 % 3, k % 3
+        j = 2 - dx
+        if dz < 2:
+            return packed(dy * 3 * C + j * C, C), dz
+        base = 9 * C + dy * 96
+        if j == 0:
+            return packed(base, C), 0
+        if j == 2:
+            return packed(base + 32, C), 1
+        first = packed(base + 64, 32)
+        second = pltpu.roll(packed(base, 32), C, 1)
+        return jnp.concatenate([first, second], axis=0), 0
+
+    def placed(k, half):
+        value, at = piece(k)
+        return value if at == half else pltpu.roll(value, C, 1)
+
+    for m in range(13):
+        weight[:, m * L : m * L + L] = jnp.where(low, placed(2 * m, 0), placed(2 * m + 1, 1))
+    weight[:, 13 * L :] = placed(26, 0)[:, :C]
+    rows = packed(HALF + BIAS_ROW, 16)
+    bias[...] = (rows[0:1] + rows[1:2])[:, :C]
+
+
+def finish(out_in, gfeat_in, sums, out, gfeat, gw1, gw2, gb1, gb2):
+    out[...] = out_in[...]
+    gfeat[...] = gfeat_in[...]
+    unpack(sums, 0, gw1, gb1)
+    unpack(sums, 1, gw2, gb2)
 
 
 def local(nb, ns, features, cotangent, mask, w1, b1, w2, b2):
@@ -516,6 +542,8 @@
     block2 = vmem((S * PL, L), F32)
     dma = pltpu.SemaphoreType.DMA
     scratch = [
+        vmem(features.shape, BF16),
+        vmem(w2.shape, BF16),
         field,
         field,
         field,
@@ -528,6 +556,7 @@
         block2,
         block2,
         block4,
+        block4,
         vmem((27 * C, L), F32),
         vmem((27 * C, L), F32),
         vmem((4, 3 * PL, PL), BF16),
@@ -537,12 +566,12 @@
         vmem((3, 3 * C, PL), F32),
         vmem((2, 2, HALF, L), F32),
         vmem((2, HALF, L), F32),
-        vmem((2, nq, chunk, L), F32),
-        vmem((2, nq, chunk, L), F32),
-        vmem((2, chunk, L), F32),
-        vmem((2, ns, chunk, L), F32),
-        vmem((2, chunk, L), F32),
-        vmem((2, 2, nq, chunk, L), F32),
+        vmem((2, nq, chunk, L), BF16),
+        vmem((2, nq, chunk, L), BF16),
+        vmem((2, chunk, L), BF16),
+        vmem((2, ns, chunk, L), BF16),
+        vmem((2, chunk, L), BF16),
+        vmem((2, 2, nq, chunk, L), BF16),
         dma((4, 2)),
         dma((4, 2)),
         dma((2, 2)),
@@ -551,11 +580,28 @@
         dma((2, 2, nq)),
         dma((2, ns)),
         dma((2, ns)),
+        dma((2,)),
     ]
     shape = jax.ShapeDtypeStruct
     in_vmem = pl.BlockSpec(memory_space=pltpu.VMEM)
+    anywhere = pl.BlockSpec(memory_space=pl.ANY)
+    output, grad_features, sums = pl.pallas_call(
+        functools.partial(kernel, nb, ns),
+        out_shape=[
+            shape(features.shape, BF16),
+            shape(features.shape, BF16),
+            shape((2, 2, HALF, L), BF16),
+        ],
+        in_specs=[in_vmem, anywhere, in_vmem, in_vmem, in_vmem, anywhere, in_vmem],
+        out_specs=[in_vmem] * 3,
+        scratch_shapes=scratch,
+        compiler_params=pltpu.CompilerParams(
+            collective_id=0, has_side_effects=True, vmem_limit_bytes=56 * 1024 * 1024
+        ),
+        name="residual_block",
+    )(features, cotangent, mask, w1, b1.reshape(1, C), w2, b2.reshape(1, C))
     output, grad_features, gw1, gw2, gb1, gb2 = pl.pallas_call(
-        functools.partial(kernel, nb, ns),
+        finish,
         out_shape=[
             shape(features.shape, BF16),
             shape(features.shape, BF16),
@@ -564,14 +610,10 @@
             shape((1, C), F32),
             shape((1, C), F32),
         ],
-        in_specs=[in_vmem] * 7,
+        in_specs=[in_vmem] * 3,
         out_specs=[in_vmem] * 6,
-        scratch_shapes=scratch,
-        compiler_params=pltpu.CompilerParams(
-            collective_id=0, has_side_effects=True, vmem_limit_bytes=56 * 1024 * 1024
-        ),
-        name="residual_block",
-    )(features, cotangent, mask, w1, b1.reshape(1, C), w2, b2.reshape(1, C))
+        name="finish",
+    )(output, grad_features, sums)
     return output, grad_features, gw1, gw2, gb1.reshape(C), gb2.reshape(C)
 
 

time: 89.8 us -> 66 us (0.73)
  Pallas kernels: 82.8 us -> 65.2 us
  local copies, waits for them, and re-layouts: 6.2 us -> 0 us
    pallas_call x1, Pallas kernels: 82.8 us -> 62.4 us  [local(): pl.pallas_call(functools.partial(kernel, nb, ns), out_shape=[shape(featur...]
    unnamed x16 -> x0, local copies, waits for them, and re-layouts: 6.2 us -> none
    pallas_call x0 -> x1, Pallas kernels: none -> 2.85 us  [local(): pl.pallas_call(finish, out_shape=[shape(features.shape, BF16), shape(feat...]
where the time goes in v2:
time: 66 us; the launch traced here: 65.9 us
  Pallas kernels  65.2 us (99%)
    pallas_call x1, Pallas kernels, local(): pl.pallas_call(functools.partial(kernel, nb, ns), out_shape=[shape(featur...  62.4 us
    pallas_call x1, Pallas kernels, local(): pl.pallas_call(finish, out_shape=[shape(features.shape, BF16), shape(feat...  2.85 us

profile of v2, /device:TPU:1, one launch (start us, length us, event | category | flops | bytes accessed | tf_op | source)
XLA Modules:
  0.0 65.9 jit_solution(16108919905334450520)
XLA Ops:
  0.6 62.4 %residual_block.1 = (bf16[1,8,64,512]{3,2,1,0:T(8,128)(2,1)}, bf16[1,8,64,512]{3,2,1,0:T(8,128)(2,1)}, bf16[2,2,512,128]{3,2,1,0:T(8,128)(2,1)}) custom-call(bf16[1,8,64,512]{3,2,1,0:T(8,128)(2,1)} %feat.1, bf16[1,8,64,512]{3,2,1,0:T(8,128)(2,1)} %cot_hbm.1, s32[1,8,512]{2,1,0:T(8,128)} %mask.1, bf16[64,1728]{1,0:T(8,128)(2,1)} %w1.1, f32[1,64]{1,0:T(1,128)} %bitcast.4, ...), custom_call_target="tpu_custom_call" | custom-call | tf_op jit(solution)/shard_map/residual_block/pallas_call | solution.py:588
  63.0 2.9 %finish.1 = (bf16[1,8,64,512]{3,2,1,0:T(8,128)(2,1)}, bf16[1,8,64,512]{3,2,1,0:T(8,128)(2,1)}, f32[64,1728]{1,0:T(8,128)}, f32[64,1728]{1,0:T(8,128)}, f32[1,64]{1,0:T(1,128)}, /*index=5*/f32[1,64]{1,0:T(1,128)}) custom-call(bf16[1,8,64,512]{3,2,1,0:T(8,128)(2,1)} %get-tuple-element.15.out_in, bf16[1,8,64,512]{3,2,1,0:T(8,128)(2,1)} %get-tuple-element.16.gfeat_in, ...), custom_call_target="tpu_custom_call" | custom-call | tf_op jit(solution)/shard_map/finish/pallas_call | solution.py:603

commit v3 on v2

--- a/solution.py
+++ b/solution.py
@@ -89,6 +89,7 @@
     halo_out,
     halo_in,
     halo_wide,
+    added,
     grads,
     pack,
     part1,
@@ -117,11 +118,33 @@
     above = lax.rem(b + 1, nb)
     other = b + 1 - 2 * core
 
+    nx = 4 if nq % 4 == 0 else nq
+    ny = nq // nx
+    cx, cy = lax.rem(q, nx), q // nx
+
+    def far(step, size):
+        return min(step, size - step)
+
+    chip_steps = [(dy, dx) for dy in range(ny) for dx in range(nx)][1:]
+    chip_steps = [None] + sorted(chip_steps, key=lambda t: -far(t[0], ny) - far(t[1], nx))
+    scene_steps = [None] + sorted(range(1, ns), key=lambda t: -far(t, ns))
+
+    def chip_to(j):
+        dy, dx = chip_steps[j]
+        return lax.rem(cy + dy, ny) * nx + lax.rem(cx + dx, nx)
+
+    def chip_from(j):
+        dy, dx = chip_steps[j]
+        return lax.rem(cy + ny - dy, ny) * nx + lax.rem(cx + nx - dx, nx)
+
     def chip_at(j):
-        return {"bricks": 2 * lax.rem(q + j, nq) + core}
+        return {"bricks": 2 * chip_to(j) + core}
 
     def scene_at(j):
-        return {"scenes": lax.rem(s + j, ns)}
+        return {"scenes": lax.rem(s + scene_steps[j], ns)}
+
+    def scene_from(j):
+        return lax.rem(s + ns - scene_steps[j], ns)
 
     cot_load = pltpu.make_async_copy(cot_hbm, cot, load_sem.at[0])
     w2_load = pltpu.make_async_copy(w2_hbm, w2, load_sem.at[1])
@@ -237,8 +260,23 @@
             exists = (b > 0) if way == 0 else (b < nb - 1)
             got = got * jnp.where(exists, 1.0, 0.0)
             swapped = pltpu.roll(got, C, 1)
-            halo_wide[way, : PL // 2, :] = jnp.where(low_half, got, swapped)
-            halo_wide[way, PL // 2 :, :] = jnp.where(low_half, swapped, got)
+            halo_wide[field, way, : PL // 2, :] = jnp.where(low_half, got, swapped)
+            halo_wide[field, way, PL // 2 :, :] = jnp.where(low_half, swapped, got)
+
+    def add_halo(field, number):
+        for way in range(2):
+            plane = halo_wide[field, way]
+            down = jnp.where(z_of == 0, 0.0, pltpu.roll(plane, 1, 0))
+            up = jnp.where(z_of == S - 1, 0.0, pltpu.roll(plane, PL - 1, 0))
+            rows = jnp.concatenate([jnp.where(low_plane, down, plane), up], axis=1).astype(BF16)
+            taps = [wa[number, e * PL + 2 * C * way : e * PL + 2 * C * way + C, :] for e in range(3)]
+            taps = jnp.concatenate(taps + [jnp.zeros((C, PL), BF16)], axis=0)
+            got = dot_nn(rows, taps)
+            edge = jnp.zeros((S, L), F32)
+            left = jnp.concatenate([edge, got[: PL - S, :L]], axis=0)
+            right = jnp.concatenate([got[S:, :L], edge], axis=0)
+            sides = jnp.where(low_plane, left, right)
+            added[way] = sides + pltpu.roll(sides, C, 1) + got[:, L:]
 
     low_plane = low_lanes(PL)
     z_of = lax.broadcasted_iota(jnp.int32, (PL, L), 0) & (S - 1)
@@ -246,17 +284,27 @@
     def rows_of(x):
         return slice(x * PL, x * PL + PL)
 
-    def fill(field):
+    def spread(ref, x):
+        rows = ref[x * S : x * S + S, :]
+        return jnp.broadcast_to(rows[:, None, :], (S, S, L)).reshape(PL, L)
+
+    def fill(field, x, u):
+        down = jnp.where(z_of == 0, 0.0, pltpu.roll(u, 1, 0))
+        up = jnp.where(z_of == S - 1, 0.0, pltpu.roll(u, PL - 1, 0))
+        tile = jnp.where(low_plane, down, u)
+        field[x, 1 : S + 1, :, :L] = tile.reshape(S, S, L).astype(BF16)
+        field[x, 1 : S + 1, :, L:] = up.reshape(S, S, L).astype(BF16)
+
+    def fill_halo(field, number):
+        below_at = (z_of == 0) & low_plane
+        above_at = z_of == S - 1
         for x in range(S):
-            u = us[rows_of(x), :]
-            at = slice(x * S, x * S + S)
-            low_z = jnp.broadcast_to(halo_wide[0, at, :][:, None, :], (S, S, L)).reshape(PL, L)
-            high_z = jnp.broadcast_to(halo_wide[1, at, :][:, None, :], (S, S, L)).reshape(PL, L)
-            down = jnp.where(z_of == 0, low_z, pltpu.roll(u, 1, 0))
-            up = jnp.where(z_of == S - 1, high_z, pltpu.roll(u, PL - 1, 0))
-            tile = jnp.where(low_plane, down, u)
+            tile = field[x, 1 : S + 1, :, :L].reshape(PL, L).astype(F32)
+            tile = jnp.where(below_at, spread(halo_wide.at[number, 0], x), tile)
             field[x, 1 : S + 1, :, :L] = tile.reshape(S, S, L).astype(BF16)
-            field[x, 1 : S + 1, :, L:] = up.reshape(S, S, L).astype(BF16)
+            tile = field[x, 1 : S + 1, :, L:].reshape(PL, L).astype(F32)
+            tile = jnp.where(above_at, spread(halo_wide.at[number, 1], x), tile)
+            field[x, 1 : S + 1, :, L:] = tile.reshape(S, S, L).astype(BF16)
 
     def conv(field, number):
         rows = jnp.concatenate([field[:, e : e + S].reshape(S * PL, PL) for e in range(3)], axis=1)
@@ -264,7 +312,9 @@
 
     def conv_result(x):
         sides = jnp.where(low_plane, yy[x, :, :L], yy[x + 2, :, :L])
-        return sides + pltpu.roll(sides, C, 1) + yy[x + 1, :, L:]
+        outer = jnp.where(z_of == 0, spread(added.at[0], x), spread(added.at[1], x))
+        outer = jnp.where((z_of == 0) | (z_of == S - 1), outer, 0.0)
+        return sides + pltpu.roll(sides, C, 1) + yy[x + 1, :, L:] + outer
 
     def turn(x, value):
         gt[(x + 1) * C : (x + 2) * C, :] = dot_nt(eye64w, value).astype(BF16)
@@ -304,7 +354,7 @@
 
     def reduce_chips_copy(number, j):
         return copy_to(
-            sum1.at[number, lax.rem(q + j, nq)],
+            sum1.at[number, chip_to(j)],
             part2.at[number, j],
             chip_send.at[number, 0, j],
             chip_recv.at[number, 0, j],
@@ -353,7 +403,7 @@
 
     def gather_chips(number):
         for j in range(1, ns):
-            scene_copy(number, j, lax.rem(s + ns - j, ns)).wait_recv()
+            scene_copy(number, j, scene_from(j)).wait_recv()
         total = part3[number, 0].astype(F32)
         for j in range(1, ns):
             total += part3[number, j].astype(F32)
@@ -365,7 +415,7 @@
 
     def gather_pair(number):
         for j in range(1, nq):
-            gather_chips_copy(number, j, lax.rem(q + nq - j, nq)).wait_recv()
+            gather_chips_copy(number, j, chip_from(j)).wait_recv()
         pair_copy(number, 1).start()
 
     def sum_end(number):
@@ -394,12 +444,20 @@
         load_features(column)
     for x in range(S):
         us[rows_of(x), :] = u0[x].reshape(PL, L)
+        fill(f0, x, u0[x].reshape(PL, L))
     pl.semaphore_wait(barrier, 2 + (nq - 1) + (ns - 1))
     send_halo(0)
     prepare_weights(w1, 0, True)
+    conv(f0, 0)
+    w2_load.wait()
+    prepare_weights(w2, 1, True)
+    prepare_weights(w2, 2, False)
+    prepare_weights(w1, 3, False)
+    cot_load.wait()
+    for column in range(4):
+        load_cotangent(column)
     receive_halo(0)
-    fill(f0)
-    conv(f0, 0)
+    add_halo(0, 0)
 
     def after_first(x):
         live = mm[x].reshape(PL, L)
@@ -408,21 +466,17 @@
         sig = sigmoid(first)
         hidden = first * sig
         sl[rows_of(x), :] = live * (sig + hidden * (1.0 - sig))
-        us[rows_of(x), :] = hidden.astype(BF16).astype(F32)
+        hidden = hidden.astype(BF16).astype(F32)
+        us[rows_of(x), :] = hidden
+        fill(f1, x, hidden)
 
     for x in range(S):
         after_first(x)
     send_halo(1)
-    w2_load.wait()
-    prepare_weights(w2, 1, True)
-    prepare_weights(w2, 2, False)
-    prepare_weights(w1, 3, False)
-    cot_load.wait()
-    for column in range(4):
-        load_cotangent(column)
+    conv(f1, 1)
+    fill_halo(f0, 0)
     receive_halo(1)
-    fill(f1)
-    conv(f1, 1)
+    add_halo(1, 1)
 
     def after_second(x):
         live = mm[x].reshape(PL, L)
@@ -437,6 +491,7 @@
         grad = grad.astype(F32)
         us[rows_of(x), :] = grad
         gs[rows_of(x), :] = grad
+        fill(f2, x, grad)
         return jnp.sum(grad.reshape(PL // 8, 8, L), axis=0)
 
     total = jnp.zeros((8, L), F32)
@@ -444,18 +499,19 @@
         total += after_second(x)
     send_halo(2)
     pack_bias(1, total)
+    conv(f2, 2)
+    fill_halo(f1, 1)
     weight_grad(f1, 1)
     sum_start(1)
     receive_halo(2)
-    fill(f2)
-    conv(f2, 2)
-    sum_chips(1)
+    add_halo(2, 2)
 
     def after_third(x):
         grad = (conv_result(x) * sl[rows_of(x), :]).astype(BF16)
         turn(x, grad)
         grad = grad.astype(F32)
         us[rows_of(x), :] = grad
+        fill(f2, x, grad)
         return jnp.sum(grad.reshape(PL // 8, 8, L), axis=0)
 
     total = jnp.zeros((8, L), F32)
@@ -463,26 +519,27 @@
         total += after_third(x)
     send_halo(3)
     pack_bias(0, total)
+    sum_chips(1)
     weight_grad(f0, 0)
     sum_start(0)
+    conv(f2, 3)
+    sum_chips(0)
     sum_scenes(1)
-    sum_chips(0)
     receive_halo(3)
-    fill(f2)
-    conv(f2, 3)
+    add_halo(3, 3)
 
     def after_fourth(x):
         value = mm[x].reshape(PL, L) * (gs[rows_of(x), :] + conv_result(x))
         o2[x] = value.reshape(S, S, L)
 
-    gather_chips(1)
     store_bricks(oo, out)
-    sum_scenes(0)
     for x in range(S):
         after_fourth(x)
+    sum_scenes(0)
+    gather_chips(1)
+    store_bricks(o2, gfeat)
+    gather_chips(0)
     gather_pair(1)
-    gather_chips(0)
-    store_bricks(o2, gfeat)
     sum_end(1)
     sums[1] = full[1].reshape(2, HALF, L)
     gather_pair(0)
@@ -526,11 +583,17 @@
     bias[...] = (rows[0:1] + rows[1:2])[:, :C]
 
 
-def finish(out_in, gfeat_in, sums, out, gfeat, gw1, gw2, gb1, gb2):
-    out[...] = out_in[...]
-    gfeat[...] = gfeat_in[...]
+def finish(out_in, gfeat_in, sums, out, gfeat, gw1, gw2, gb1, gb2, sem):
+    copies = [
+        pltpu.make_async_copy(out_in, out, sem.at[0]),
+        pltpu.make_async_copy(gfeat_in, gfeat, sem.at[1]),
+    ]
+    for copy in copies:
+        copy.start()
     unpack(sums, 0, gw1, gb1)
     unpack(sums, 1, gw2, gb2)
+    for copy in copies:
+        copy.wait()
 
 
 def local(nb, ns, features, cotangent, mask, w1, b1, w2, b2):
@@ -562,6 +625,7 @@
         vmem((4, 3 * PL, PL), BF16),
         vmem((4, 2, PL // 2, L), BF16),
         vmem((4, 2, PL // 2, L), BF16),
+        vmem((4, 2, PL, L), F32),
         vmem((2, PL, L), F32),
         vmem((3, 3 * C, PL), F32),
         vmem((2, 2, HALF, L), F32),
@@ -588,9 +652,9 @@
     output, grad_features, sums = pl.pallas_call(
         functools.partial(kernel, nb, ns),
         out_shape=[
-            shape(features.shape, BF16),
-            shape(features.shape, BF16),
-            shape((2, 2, HALF, L), BF16),
+            pltpu.VMEM(features.shape, BF16),
+            pltpu.VMEM(features.shape, BF16),
+            pltpu.VMEM((2, 2, HALF, L), BF16),
         ],
         in_specs=[in_vmem, anywhere, in_vmem, in_vmem, in_vmem, anywhere, in_vmem],
         out_specs=[in_vmem] * 3,
@@ -611,7 +675,9 @@
             shape((1, C), F32),
         ],
         in_specs=[in_vmem] * 3,
-        out_specs=[in_vmem] * 6,
+        out_specs=[anywhere] * 2 + [in_vmem] * 4,
+        scratch_shapes=[dma((2,))],
+        compiler_params=pltpu.CompilerParams(vmem_limit_bytes=8 * 1024 * 1024),
         name="finish",
     )(output, grad_features, sums)
     return output, grad_features, gw1, gw2, gb1.reshape(C), gb2.reshape(C)

time: 66 us -> 61.6 us (0.933)
  Pallas kernels: 65.2 us -> 60.7 us
    pallas_call x1, Pallas kernels: 62.4 us -> 58.8 us  [local(): pl.pallas_call(functools.partial(kernel, nb, ns), out_shape=[pltpu.VMEM(f...]
    pallas_call x1, Pallas kernels: 2.85 us -> 1.91 us  [local(): pl.pallas_call(finish, out_shape=[shape(features.shape, BF16), shape(feat...]
where the time goes in v3:
time: 61.6 us; the launch traced here: 61.5 us
  Pallas kernels  60.7 us (99%)
  between operations  0.82 us (1%)
    pallas_call x1, Pallas kernels, local(): pl.pallas_call(functools.partial(kernel, nb, ns), out_shape=[pltpu.VMEM(f...  58.8 us
    pallas_call x1, Pallas kernels, local(): pl.pallas_call(finish, out_shape=[shape(features.shape, BF16), shape(feat...  1.91 us

profile of v3, /device:TPU:1, one launch (start us, length us, event | category | flops | bytes accessed | tf_op | source)
XLA Modules:
  0.0 61.5 jit_solution(6795239078263238921)
XLA Ops:
  0.6 58.8 %residual_block.1 = (bf16[1,8,64,512]{3,2,1,0:T(8,128)(2,1)S(1)}, bf16[1,8,64,512]{3,2,1,0:T(8,128)(2,1)S(1)}, bf16[2,2,512,128]{3,2,1,0:T(8,128)(2,1)S(1)}) custom-call(bf16[1,8,64,512]{3,2,1,0:T(8,128)(2,1)} %feat.1, bf16[1,8,64,512]{3,2,1,0:T(8,128)(2,1)} %cot_hbm.1, s32[1,8,512]{2,1,0:T(8,128)} %mask.1, bf16[64,1728]{1,0:T(8,128)(2,1)} %w1.1, ...), custom_call_target="tpu_custom_call" | custom-call | tf_op jit(solution)/shard_map/residual_block/pallas_call | solution.py:652
  59.4 1.9 %finish.1 = (bf16[1,8,64,512]{3,2,1,0:T(8,128)(2,1)}, bf16[1,8,64,512]{3,2,1,0:T(8,128)(2,1)}, f32[64,1728]{1,0:T(8,128)}, f32[64,1728]{1,0:T(8,128)}, f32[1,64]{1,0:T(1,128)}, /*index=5*/f32[1,64]{1,0:T(1,128)}) custom-call(bf16[1,8,64,512]{3,2,1,0:T(8,128)(2,1)S(1)} %get-tuple-element.15.out_in, bf16[1,8,64,512]{3,2,1,0:T(8,128)(2,1)S(1)} %get-tuple-element.16.gfeat_in, ...), custom_call_target="tpu_custom_call" | custom-call | tf_op jit(solution)/shard_map/finish/pallas_call | solution.py:667

commit v4 on v3

--- a/solution.py
+++ b/solution.py
@@ -307,8 +307,10 @@
             field[x, 1 : S + 1, :, L:] = tile.reshape(S, S, L).astype(BF16)
 
     def conv(field, number):
-        rows = jnp.concatenate([field[:, e : e + S].reshape(S * PL, PL) for e in range(3)], axis=1)
-        yy[1 : S + 1] = dot_nn(rows, wa[number]).reshape(S, PL, PL)
+        for x in range(0, S, 4):
+            rows = [field[x : x + 4, e : e + S].reshape(4 * PL, PL) for e in range(3)]
+            product = dot_nn(jnp.concatenate(rows, axis=1), wa[number])
+            yy[x + 1 : x + 1 + 4] = product.reshape(4, PL, PL)
 
     def conv_result(x):
         sides = jnp.where(low_plane, yy[x, :, :L], yy[x + 2, :, :L])
@@ -339,7 +341,7 @@
 
     def split_bias(value, first_row):
         row = lax.broadcasted_iota(jnp.int32, value.shape, 0) + first_row
-        at = BIAS_ROW % chunk if value.shape[0] == chunk else BIAS_ROW
+        at = BIAS_ROW % chunk
         whole = value[at : at + 1] + value[at + 1 : at + 2]
         high = whole.astype(BF16).astype(F32)
         value = jnp.where(row == HALF + BIAS_ROW, high, value)
@@ -384,8 +386,11 @@
 
     def sum_chips(number):
         pair_copy(number, 0).wait_recv()
-        total = split_bias(pack[number, core] + part1[number], core * HALF)
+        total = pack[number, core] + part1[number]
         sum1[number] = total.astype(BF16).reshape(nq, chunk, L)
+        n = BIAS_ROW // chunk
+        rows = split_bias(total[n * chunk : n * chunk + chunk], core * HALF + n * chunk)
+        sum1[number, n] = rows.astype(BF16)
         for j in range(1, nq):
             reduce_chips_copy(number, j).start()
 
@@ -423,7 +428,6 @@
 
     def sends_end(number):
         pair_copy(number, 0).wait_send()
-        pair_copy(number, 1).wait_send()
         for j in range(1, nq):
             reduce_chips_copy(number, j).wait_send()
             gather_chips_copy(number, j, q).wait_send()
@@ -522,8 +526,9 @@
     sum_chips(1)
     weight_grad(f0, 0)
     sum_start(0)
+    store_bricks(oo, out)
+    sum_chips(0)
     conv(f2, 3)
-    sum_chips(0)
     sum_scenes(1)
     receive_halo(3)
     add_halo(3, 3)
@@ -532,24 +537,25 @@
         value = mm[x].reshape(PL, L) * (gs[rows_of(x), :] + conv_result(x))
         o2[x] = value.reshape(S, S, L)
 
-    store_bricks(oo, out)
     for x in range(S):
         after_fourth(x)
     sum_scenes(0)
     gather_chips(1)
     store_bricks(o2, gfeat)
     gather_chips(0)
+    for field in range(4):
+        for way in range(2):
+            halo_copy(field, way).wait_send()
     gather_pair(1)
+    sends_end(1)
     sum_end(1)
     sums[1] = full[1].reshape(2, HALF, L)
     gather_pair(0)
-    sends_end(1)
+    pair_copy(1, 1).wait_send()
+    sends_end(0)
     sum_end(0)
     sums[0] = full[0].reshape(2, HALF, L)
-    sends_end(0)
-    for field in range(4):
-        for way in range(2):
-            halo_copy(field, way).wait_send()
+    pair_copy(0, 1).wait_send()
 
 
 def unpack(sums, number, weight, bias):

time: 61.6 us -> 57.1 us (0.927)
  Pallas kernels: 60.7 us -> 56.2 us
    pallas_call x1, Pallas kernels: 58.8 us -> 54.3 us  [local(): pl.pallas_call(functools.partial(kernel, nb, ns), out_shape=[pltpu.VMEM(f...]
where the time goes in v4:
time: 57.1 us; the launch traced here: 57 us
  Pallas kernels  56.2 us (98%)
  between operations  0.8 us (1%)
    pallas_call x1, Pallas kernels, local(): pl.pallas_call(functools.partial(kernel, nb, ns), out_shape=[pltpu.VMEM(f...  54.3 us
    pallas_call x1, Pallas kernels, local(): pl.pallas_call(finish, out_shape=[shape(features.shape, BF16), shape(feat...  1.91 us

profile of v4, /device:TPU:1, one launch (start us, length us, event | category | flops | bytes accessed | tf_op | source)
XLA Modules:
  0.0 57.0 jit_solution(14612383024895751425)
XLA Ops:
  0.6 54.3 %residual_block.1 = (bf16[1,8,64,512]{3,2,1,0:T(8,128)(2,1)S(1)}, bf16[1,8,64,512]{3,2,1,0:T(8,128)(2,1)S(1)}, bf16[2,2,512,128]{3,2,1,0:T(8,128)(2,1)S(1)}) custom-call(bf16[1,8,64,512]{3,2,1,0:T(8,128)(2,1)} %feat.1, bf16[1,8,64,512]{3,2,1,0:T(8,128)(2,1)} %cot_hbm.1, s32[1,8,512]{2,1,0:T(8,128)} %mask.1, bf16[64,1728]{1,0:T(8,128)(2,1)} %w1.1, ...), custom_call_target="tpu_custom_call" | custom-call | tf_op jit(solution)/shard_map/residual_block/pallas_call | solution.py:658
  54.9 1.9 %finish.1 = (bf16[1,8,64,512]{3,2,1,0:T(8,128)(2,1)}, bf16[1,8,64,512]{3,2,1,0:T(8,128)(2,1)}, f32[64,1728]{1,0:T(8,128)}, f32[64,1728]{1,0:T(8,128)}, f32[1,64]{1,0:T(1,128)}, /*index=5*/f32[1,64]{1,0:T(1,128)}) custom-call(bf16[1,8,64,512]{3,2,1,0:T(8,128)(2,1)S(1)} %get-tuple-element.15.out_in, bf16[1,8,64,512]{3,2,1,0:T(8,128)(2,1)S(1)} %get-tuple-element.16.gfeat_in, ...), custom_call_target="tpu_custom_call" | custom-call | tf_op jit(solution)/shard_map/finish/pallas_call | solution.py:673

commit v5 on v4

--- a/solution.py
+++ b/solution.py
@@ -58,18 +58,23 @@
 def kernel(
     nb,
     ns,
-    feat,
+    feat_hbm,
     cot_hbm,
-    mask,
-    w1,
-    b1,
+    mask_hbm,
+    w1_hbm,
+    b1_hbm,
     w2_hbm,
-    b2,
+    b2_hbm,
     out,
     gfeat,
     sums,
     cot,
     w2,
+    feat,
+    mask,
+    w1,
+    b1,
+    b2,
     f0,
     f1,
     f2,
@@ -148,8 +153,13 @@
 
     cot_load = pltpu.make_async_copy(cot_hbm, cot, load_sem.at[0])
     w2_load = pltpu.make_async_copy(w2_hbm, w2, load_sem.at[1])
-    cot_load.start()
-    w2_load.start()
+    feat_load = pltpu.make_async_copy(feat_hbm, feat, load_sem.at[2])
+    mask_load = pltpu.make_async_copy(mask_hbm, mask, load_sem.at[3])
+    w1_load = pltpu.make_async_copy(w1_hbm, w1, load_sem.at[4])
+    b1_load = pltpu.make_async_copy(b1_hbm, b1, load_sem.at[5])
+    b2_load = pltpu.make_async_copy(b2_hbm, b2, load_sem.at[6])
+    feat_load.start()
+    mask_load.start()
 
     barrier = pltpu.get_barrier_semaphore()
 
@@ -162,6 +172,9 @@
         greet(chip_at(j))
     for j in range(1, ns):
         greet(scene_at(j))
+
+    for load in (w1_load, w2_load, b1_load, b2_load, cot_load):
+        load.start()
 
     eye256 = eye(PL, PL)
     eye128 = eye(L, L)
@@ -444,6 +457,8 @@
     for number in range(2):
         pack[number, 1, BIAS_ROW:, :] = jnp.zeros((HALF - BIAS_ROW, L), F32)
 
+    feat_load.wait()
+    mask_load.wait()
     for column in range(4):
         load_features(column)
     for x in range(S):
@@ -451,9 +466,12 @@
         fill(f0, x, u0[x].reshape(PL, L))
     pl.semaphore_wait(barrier, 2 + (nq - 1) + (ns - 1))
     send_halo(0)
+    w1_load.wait()
     prepare_weights(w1, 0, True)
     conv(f0, 0)
     w2_load.wait()
+    b1_load.wait()
+    b2_load.wait()
     prepare_weights(w2, 1, True)
     prepare_weights(w2, 2, False)
     prepare_weights(w1, 3, False)
@@ -613,6 +631,11 @@
     scratch = [
         vmem(features.shape, BF16),
         vmem(w2.shape, BF16),
+        vmem(features.shape, BF16),
+        vmem(mask.shape, jnp.int32),
+        vmem(w1.shape, BF16),
+        vmem((1, C), F32),
+        vmem((1, C), F32),
         field,
         field,
         field,
@@ -650,7 +673,7 @@
         dma((2, 2, nq)),
         dma((2, ns)),
         dma((2, ns)),
-        dma((2,)),
+        dma((7,)),
     ]
     shape = jax.ShapeDtypeStruct
     in_vmem = pl.BlockSpec(memory_space=pltpu.VMEM)
@@ -662,7 +685,7 @@
             pltpu.VMEM(features.shape, BF16),
             pltpu.VMEM((2, 2, HALF, L), BF16),
         ],
-        in_specs=[in_vmem, anywhere, in_vmem, in_vmem, in_vmem, anywhere, in_vmem],
+        in_specs=[anywhere] * 7,
         out_specs=[in_vmem] * 3,
         scratch_shapes=scratch,
         compiler_params=pltpu.CompilerParams(

time: 57.1 us -> 56.1 us (0.982)
  Pallas kernels: 56.2 us -> 55.2 us
    pallas_call x1, Pallas kernels: 54.3 us -> 53.3 us  [local(): pl.pallas_call(functools.partial(kernel, nb, ns), out_shape=[pltpu.VMEM(f...]
where the time goes in v5:
time: 56.1 us; the launch traced here: 56 us
  Pallas kernels  55.2 us (98%)
  between operations  0.8 us (1%)
    pallas_call x1, Pallas kernels, local(): pl.pallas_call(functools.partial(kernel, nb, ns), out_shape=[pltpu.VMEM(f...  53.3 us
    pallas_call x1, Pallas kernels, local(): pl.pallas_call(finish, out_shape=[shape(features.shape, BF16), shape(feat...  1.91 us

profile of v5, /device:TPU:1, one launch (start us, length us, event | category | flops | bytes accessed | tf_op | source)
XLA Modules:
  0.0 56.0 jit_solution(5860503421385415666)
XLA Ops:
  0.6 53.3 %residual_block.1 = (bf16[1,8,64,512]{3,2,1,0:T(8,128)(2,1)S(1)}, bf16[1,8,64,512]{3,2,1,0:T(8,128)(2,1)S(1)}, bf16[2,2,512,128]{3,2,1,0:T(8,128)(2,1)S(1)}) custom-call(bf16[1,8,64,512]{3,2,1,0:T(8,128)(2,1)} %feat_hbm.1, bf16[1,8,64,512]{3,2,1,0:T(8,128)(2,1)} %cot_hbm.1, s32[1,8,512]{2,1,0:T(8,128)} %mask_hbm.1, bf16[64,1728]{1,0:T(8,128)(2,1)} %w1_hbm.1, ...), custom_call_target="tpu_custom_call" | custom-call | tf_op jit(solution)/shard_map/residual_block/pallas_call | solution.py:681
  54.0 1.9 %finish.1 = (bf16[1,8,64,512]{3,2,1,0:T(8,128)(2,1)}, bf16[1,8,64,512]{3,2,1,0:T(8,128)(2,1)}, f32[64,1728]{1,0:T(8,128)}, f32[64,1728]{1,0:T(8,128)}, f32[1,64]{1,0:T(1,128)}, /*index=5*/f32[1,64]{1,0:T(1,128)}) custom-call(bf16[1,8,64,512]{3,2,1,0:T(8,128)(2,1)S(1)} %get-tuple-element.15.out_in, bf16[1,8,64,512]{3,2,1,0:T(8,128)(2,1)S(1)} %get-tuple-element.16.gfeat_in, ...), custom_call_target="tpu_custom_call" | custom-call | tf_op jit(solution)/shard_map/finish/pallas_call | solution.py:696
